TPU v7x, 256 devices: a whole 4x4x8 slice. The times are simulated.
256 devices in a mesh: tm: 32 (over y, z), gx: 4 (over x), gy: 2 (over core).
Axes of the slice: x: 4, y: 4, z: 8, core: 2. Of those that a mesh axis runs over, the one named last changes fastest.
Arguments:
- guesses: float32 [32, 64, 32, 256], P('tm', None, 'gx', 'gy'), may hold values from -6 to 6
- forcing: float32 [32, 64, 32, 256], P('tm', None, 'gx', 'gy'), may hold values from -4 to 4
- step_weight: float32 [16], replicated, may hold values from 0.25 to 1
- land_mask: int32 [32, 256], P('gx', 'gy'), may hold values 0 or 1
- fine_matrix: float32 [64, 64], replicated, may hold values from -1 to 1
- coupling: float32 [4, 64, 64], replicated, may hold values from -0.09375 to 0.09375
- coarse_matrix: float32 [64, 64], replicated, may hold values from -1 to 1
Outputs:
- updated_points: float32 [32, 64, 32, 256], P('tm', None, 'gx', 'gy')
- residual: float32 [32, 64, 32, 256], P('tm', None, 'gx', 'gy')
All inputs are finite; a program needn't handle non-finite values. No bound on the sum of `land_mask` on one device may be relied on, other than what follows from the above.
Results may differ from a plain program's by a relative error of at most 0.0003.
Values sent between devices are 32-bit elements; how exact they have to be, the bound alone decides.
A program may use at most 64 MiB of HBM per device.

v0:
```python
import jax
import jax.numpy as jnp
from jax import lax
from jax.sharding import PartitionSpec as P


def passed_along(value, axis, steps):
    count = lax.axis_size(axis)
    initial, last = (max(0, -steps), min(count, count - steps))
    return lax.ppermute(value, axis, [(source, source + steps) for source in range(initial, last)])


def padded_2(cells, sides, width):
    for axis, dim in sides:
        count = lax.axis_size(axis)
        ends = count - 1
        head = lax.slice_in_dim(cells, 0, width, axis=dim)
        tail = lax.slice_in_dim(cells, cells.shape[dim] - width, cells.shape[dim], axis=dim)
        cells = jnp.concatenate(
            [
                lax.ppermute(tail, axis, [(i, (i + 1) % count) for i in range(ends)]),
                cells,
                lax.ppermute(head, axis, [((i + 1) % count, i) for i in range(ends)]),
            ],
            axis=dim,
        )
    return cells


def propagate(matrix, field):
    return jnp.einsum("ij,jxy->ixy", matrix, field, precision=lax.Precision.HIGHEST)


def batched(matrix, field):
    return jnp.einsum("ij,cjxy->cixy", matrix, field, precision=lax.Precision.HIGHEST)


def local_step(padded, source, fine_matrix, coupling, ocean_mask):
    summed = batched(fine_matrix, padded[:, :, 1:-1, 1:-1])
    summed = summed + batched(coupling[0], padded[:, :, :-2, 1:-1])
    summed = summed + batched(coupling[1], padded[:, :, 2:, 1:-1])
    summed = summed + batched(coupling[2], padded[:, :, 1:-1, :-2])
    summed = summed + batched(coupling[3], padded[:, :, 1:-1, 2:])
    return (summed + source) * ocean_mask


def per_device(guesses, forcing, step_weight, land_mask, fine_matrix, coupling, coarse_matrix):
    ocean_mask = land_mask.astype(jnp.float32)[None, None]
    plane_mask = ocean_mask[0]
    count = guesses.shape[0]
    steps_total = step_weight.shape[0]
    successor = passed_along(guesses[0], "tm", -1)
    starts = jnp.concatenate([guesses[1:], successor[None]], 0)
    adjoint = starts
    for step_index in range(steps_total - 1, -1, -1):
        padded = padded_2(adjoint, (("gx", 2), ("gy", 3)), 1)
        adjoint = local_step(
            padded, step_weight[step_index] * forcing, fine_matrix, coupling, ocean_mask
        )
    residual = adjoint - guesses * ocean_mask

    def advance(matrix, field):
        return propagate(matrix, field) * plane_mask

    offset = jnp.zeros_like(guesses[0])
    interval = 0
    offset = advance(coarse_matrix, offset) + residual[interval]

    def relay_turn(turn, incoming):
        return passed_along(advance(coarse_matrix, incoming) + offset, "tm", -1)

    incoming = lax.fori_loop(0, lax.axis_size("tm") - 1, relay_turn, jnp.zeros_like(offset))
    correction = incoming
    corrections = [None] * count
    interval = 0
    correction = advance(coarse_matrix, correction) + residual[interval]
    corrections[interval] = correction
    return (guesses + jnp.stack(corrections, 0), residual)


def solution(mesh):
    return jax.shard_map(
        per_device,
        mesh=mesh,
        in_specs=(
            P("tm", None, "gx", "gy"),
            P("tm", None, "gx", "gy"),
            P(),
            P("gx", "gy"),
            P(),
            P(),
            P(),
        ),
        out_specs=(P("tm", None, "gx", "gy"), P("tm", None, "gx", "gy")),
        check_vma=False,
    )
```

profile of v0, /device:TPU:24, one launch (start us, length us, event | category | flops | bytes accessed | tf_op | source)
XLA Modules:
  0.0 609.7 jit_solution(17396817896490975098)
XLA Ops:
  1.7 7.9 %collective-permute-start.1 = (f32[64,8,128]{2,0,1:T(8,128)S(1)}, f32[64,8,128]{2,0,1:T(8,128)S(1)}, u32[]{:S(2)}, u32[]{:S(2)}) collective-permute-start(f32[64,8,128]{2,0,1:T(8,128)S(1)} %bitcast.601), channel_id=1, source_target_pairs={{8,0},{16,8},{24,16},{32,24},{40,32},{48,40},{56,48},{64,56},{72,6... | collective-permute-start | bytes 786440 | tf_op jit(solution)/shard_map/ppermute | solution.py:10
  9.6 5.5 collective-permute-done.1
  36.3 4.1 collective-permute-done.7
  51.9 4.1 collective-permute-done.11
  66.2 4.1 collective-permute-done.15
  80.6 4.1 collective-permute-done.19
  109.3 4.1 collective-permute-done.27
  123.7 4.1 collective-permute-done.31
  138.1 4.1 collective-permute-done.35
  152.6 4.1 collective-permute-done.39
  166.9 4.1 collective-permute-done.43
  181.2 4.1 collective-permute-done.47
  195.7 4.1 collective-permute-done.51
  210.0 4.1 collective-permute-done.55
  224.4 4.1 collective-permute-done.59
  238.8 4.1 collective-permute-done.63
  250.7 357.5 %while.10 = (s32[]{:T(128)}, f32[64,8,128]{2,0,1:T(8,128)S(1)}, f32[64,64]{1,0:T(8,128)S(1)}, f32[1,8,128]{2,1,0:T(8,128)S(1)}, f32[64,8,128]{2,0,1:T(8,128)S(1)}, /*index=5*/s32[]{:T(128)}) while((s32[]{:T(128)}, f32[64,8,128]{2,0,1:T(8,128)S(1)}, f32[64,64]{1,0:T(8,128)S(1)}, f32[1,8,128]{2,1,0:T(8,128)S(1)}, f32[64,8,128]{2,0,1:T(8,128)S(1)}, ...), condition=%wide.region_1.0_spmd, body=%wide.region_0.0_spmd.sunk | while | flops 50462720 | bytes 1855597 | solution.py:72
  251.1 6.4 %collective-permute-start = (f32[64,8,128]{2,0,1:T(8,128)S(1)}, f32[64,8,128]{2,0,1:T(8,128)S(1)}, u32[]{:S(2)}, u32[]{:S(2)}) collective-permute-start(f32[64,8,128]{2,0,1:T(8,128)S(1)} %fusion.600), channel_id=1, source_target_pairs={{8,0},{16,8},{24,16},{32,24},{40,32},{48,40},{56,48},{64,56},{72,6... | collective-permute-start | bytes 786440 | tf_op jit(solution)/shard_map/while/body/eval_jaxpr/ppermute | solution.py:10
  257.5 6.1 collective-permute-done
  264.0 6.5 %collective-permute-start = (f32[64,8,128]{2,0,1:T(8,128)S(1)}, f32[64,8,128]{2,0,1:T(8,128)S(1)}, u32[]{:S(2)}, u32[]{:S(2)}) collective-permute-start(f32[64,8,128]{2,0,1:T(8,128)S(1)} %fusion.600), channel_id=1, source_target_pairs={{8,0},{16,8},{24,16},{32,24},{40,32},{48,40},{56,48},{64,56},{72,6... | collective-permute-start | bytes 786440 | tf_op jit(solution)/shard_map/while/body/eval_jaxpr/ppermute | solution.py:10
  270.5 5.3 collective-permute-done
  276.1 6.5 %collective-permute-start = (f32[64,8,128]{2,0,1:T(8,128)S(1)}, f32[64,8,128]{2,0,1:T(8,128)S(1)}, u32[]{:S(2)}, u32[]{:S(2)}) collective-permute-start(f32[64,8,128]{2,0,1:T(8,128)S(1)} %fusion.600), channel_id=1, source_target_pairs={{8,0},{16,8},{24,16},{32,24},{40,32},{48,40},{56,48},{64,56},{72,6... | collective-permute-start | bytes 786440 | tf_op jit(solution)/shard_map/while/body/eval_jaxpr/ppermute | solution.py:10
  282.6 4.4 collective-permute-done
  287.4 6.5 %collective-permute-start = (f32[64,8,128]{2,0,1:T(8,128)S(1)}, f32[64,8,128]{2,0,1:T(8,128)S(1)}, u32[]{:S(2)}, u32[]{:S(2)}) collective-permute-start(f32[64,8,128]{2,0,1:T(8,128)S(1)} %fusion.600), channel_id=1, source_target_pairs={{8,0},{16,8},{24,16},{32,24},{40,32},{48,40},{56,48},{64,56},{72,6... | collective-permute-start | bytes 786440 | tf_op jit(solution)/shard_map/while/body/eval_jaxpr/ppermute | solution.py:10
  298.1 6.5 %collective-permute-start = (f32[64,8,128]{2,0,1:T(8,128)S(1)}, f32[64,8,128]{2,0,1:T(8,128)S(1)}, u32[]{:S(2)}, u32[]{:S(2)}) collective-permute-start(f32[64,8,128]{2,0,1:T(8,128)S(1)} %fusion.600), channel_id=1, source_target_pairs={{8,0},{16,8},{24,16},{32,24},{40,32},{48,40},{56,48},{64,56},{72,6... | collective-permute-start | bytes 786440 | tf_op jit(solution)/shard_map/while/body/eval_jaxpr/ppermute | solution.py:10
  308.9 6.5 %collective-permute-start = (f32[64,8,128]{2,0,1:T(8,128)S(1)}, f32[64,8,128]{2,0,1:T(8,128)S(1)}, u32[]{:S(2)}, u32[]{:S(2)}) collective-permute-start(f32[64,8,128]{2,0,1:T(8,128)S(1)} %fusion.600), channel_id=1, source_target_pairs={{8,0},{16,8},{24,16},{32,24},{40,32},{48,40},{56,48},{64,56},{72,6... | collective-permute-start | bytes 786440 | tf_op jit(solution)/shard_map/while/body/eval_jaxpr/ppermute | solution.py:10
  319.6 6.5 %collective-permute-start = (f32[64,8,128]{2,0,1:T(8,128)S(1)}, f32[64,8,128]{2,0,1:T(8,128)S(1)}, u32[]{:S(2)}, u32[]{:S(2)}) collective-permute-start(f32[64,8,128]{2,0,1:T(8,128)S(1)} %fusion.600), channel_id=1, source_target_pairs={{8,0},{16,8},{24,16},{32,24},{40,32},{48,40},{56,48},{64,56},{72,6... | collective-permute-start | bytes 786440 | tf_op jit(solution)/shard_map/while/body/eval_jaxpr/ppermute | solution.py:10
  330.3 6.5 %collective-permute-start = (f32[64,8,128]{2,0,1:T(8,128)S(1)}, f32[64,8,128]{2,0,1:T(8,128)S(1)}, u32[]{:S(2)}, u32[]{:S(2)}) collective-permute-start(f32[64,8,128]{2,0,1:T(8,128)S(1)} %fusion.600), channel_id=1, source_target_pairs={{8,0},{16,8},{24,16},{32,24},{40,32},{48,40},{56,48},{64,56},{72,6... | collective-permute-start | bytes 786440 | tf_op jit(solution)/shard_map/while/body/eval_jaxpr/ppermute | solution.py:10
  336.9 4.8 collective-permute-done
  342.0 6.5 %collective-permute-start = (f32[64,8,128]{2,0,1:T(8,128)S(1)}, f32[64,8,128]{2,0,1:T(8,128)S(1)}, u32[]{:S(2)}, u32[]{:S(2)}) collective-permute-start(f32[64,8,128]{2,0,1:T(8,128)S(1)} %fusion.600), channel_id=1, source_target_pairs={{8,0},{16,8},{24,16},{32,24},{40,32},{48,40},{56,48},{64,56},{72,6... | collective-permute-start | bytes 786440 | tf_op jit(solution)/shard_map/while/body/eval_jaxpr/ppermute | solution.py:10
  348.5 6.0 collective-permute-done
  354.9 6.5 %collective-permute-start = (f32[64,8,128]{2,0,1:T(8,128)S(1)}, f32[64,8,128]{2,0,1:T(8,128)S(1)}, u32[]{:S(2)}, u32[]{:S(2)}) collective-permute-start(f32[64,8,128]{2,0,1:T(8,128)S(1)} %fusion.600), channel_id=1, source_target_pairs={{8,0},{16,8},{24,16},{32,24},{40,32},{48,40},{56,48},{64,56},{72,6... | collective-permute-start | bytes 786440 | tf_op jit(solution)/shard_map/while/body/eval_jaxpr/ppermute | solution.py:10
  361.4 6.2 %collective-permute-done = f32[64,8,128]{2,0,1:T(8,128)S(1)} collective-permute-done((f32[64,8,128]{2,0,1:T(8,128)S(1)}, f32[64,8,128]{2,0,1:T(8,128)S(1)}, u32[]{:S(2)}, u32[]{:S(2)}) %collective-permute-start) | collective-permute-done | bytes 262176 | tf_op jit(solution)/shard_map/while/body/eval_jaxpr/ppermute | solution.py:10
  368.0 6.5 %collective-permute-start = (f32[64,8,128]{2,0,1:T(8,128)S(1)}, f32[64,8,128]{2,0,1:T(8,128)S(1)}, u32[]{:S(2)}, u32[]{:S(2)}) collective-permute-start(f32[64,8,128]{2,0,1:T(8,128)S(1)} %fusion.600), channel_id=1, source_target_pairs={{8,0},{16,8},{24,16},{32,24},{40,32},{48,40},{56,48},{64,56},{72,6... | collective-permute-start | bytes 786440 | tf_op jit(solution)/shard_map/while/body/eval_jaxpr/ppermute | solution.py:10
  374.5 5.4 collective-permute-done
  380.3 6.5 %collective-permute-start = (f32[64,8,128]{2,0,1:T(8,128)S(1)}, f32[64,8,128]{2,0,1:T(8,128)S(1)}, u32[]{:S(2)}, u32[]{:S(2)}) collective-permute-start(f32[64,8,128]{2,0,1:T(8,128)S(1)} %fusion.600), channel_id=1, source_target_pairs={{8,0},{16,8},{24,16},{32,24},{40,32},{48,40},{56,48},{64,56},{72,6... | collective-permute-start | bytes 786440 | tf_op jit(solution)/shard_map/while/body/eval_jaxpr/ppermute | solution.py:10
  386.8 4.6 collective-permute-done
  391.7 6.5 %collective-permute-start = (f32[64,8,128]{2,0,1:T(8,128)S(1)}, f32[64,8,128]{2,0,1:T(8,128)S(1)}, u32[]{:S(2)}, u32[]{:S(2)}) collective-permute-start(f32[64,8,128]{2,0,1:T(8,128)S(1)} %fusion.600), channel_id=1, source_target_pairs={{8,0},{16,8},{24,16},{32,24},{40,32},{48,40},{56,48},{64,56},{72,6... | collective-permute-start | bytes 786440 | tf_op jit(solution)/shard_map/while/body/eval_jaxpr/ppermute | solution.py:10
  402.4 6.5 %collective-permute-start = (f32[64,8,128]{2,0,1:T(8,128)S(1)}, f32[64,8,128]{2,0,1:T(8,128)S(1)}, u32[]{:S(2)}, u32[]{:S(2)}) collective-permute-start(f32[64,8,128]{2,0,1:T(8,128)S(1)} %fusion.600), channel_id=1, source_target_pairs={{8,0},{16,8},{24,16},{32,24},{40,32},{48,40},{56,48},{64,56},{72,6... | collective-permute-start | bytes 786440 | tf_op jit(solution)/shard_map/while/body/eval_jaxpr/ppermute | solution.py:10
  413.2 6.5 %collective-permute-start = (f32[64,8,128]{2,0,1:T(8,128)S(1)}, f32[64,8,128]{2,0,1:T(8,128)S(1)}, u32[]{:S(2)}, u32[]{:S(2)}) collective-permute-start(f32[64,8,128]{2,0,1:T(8,128)S(1)} %fusion.600), channel_id=1, source_target_pairs={{8,0},{16,8},{24,16},{32,24},{40,32},{48,40},{56,48},{64,56},{72,6... | collective-permute-start | bytes 786440 | tf_op jit(solution)/shard_map/while/body/eval_jaxpr/ppermute | solution.py:10
  423.9 6.5 %collective-permute-start = (f32[64,8,128]{2,0,1:T(8,128)S(1)}, f32[64,8,128]{2,0,1:T(8,128)S(1)}, u32[]{:S(2)}, u32[]{:S(2)}) collective-permute-start(f32[64,8,128]{2,0,1:T(8,128)S(1)} %fusion.600), channel_id=1, source_target_pairs={{8,0},{16,8},{24,16},{32,24},{40,32},{48,40},{56,48},{64,56},{72,6... | collective-permute-start | bytes 786440 | tf_op jit(solution)/shard_map/while/body/eval_jaxpr/ppermute | solution.py:10
  434.7 6.5 %collective-permute-start = (f32[64,8,128]{2,0,1:T(8,128)S(1)}, f32[64,8,128]{2,0,1:T(8,128)S(1)}, u32[]{:S(2)}, u32[]{:S(2)}) collective-permute-start(f32[64,8,128]{2,0,1:T(8,128)S(1)} %fusion.600), channel_id=1, source_target_pairs={{8,0},{16,8},{24,16},{32,24},{40,32},{48,40},{56,48},{64,56},{72,6... | collective-permute-start | bytes 786440 | tf_op jit(solution)/shard_map/while/body/eval_jaxpr/ppermute | solution.py:10
  441.2 4.6 collective-permute-done
  446.2 6.5 %collective-permute-start = (f32[64,8,128]{2,0,1:T(8,128)S(1)}, f32[64,8,128]{2,0,1:T(8,128)S(1)}, u32[]{:S(2)}, u32[]{:S(2)}) collective-permute-start(f32[64,8,128]{2,0,1:T(8,128)S(1)} %fusion.600), channel_id=1, source_target_pairs={{8,0},{16,8},{24,16},{32,24},{40,32},{48,40},{56,48},{64,56},{72,6... | collective-permute-start | bytes 786440 | tf_op jit(solution)/shard_map/while/body/eval_jaxpr/ppermute | solution.py:10
  452.6 5.7 collective-permute-done
  458.8 6.5 %collective-permute-start = (f32[64,8,128]{2,0,1:T(8,128)S(1)}, f32[64,8,128]{2,0,1:T(8,128)S(1)}, u32[]{:S(2)}, u32[]{:S(2)}) collective-permute-start(f32[64,8,128]{2,0,1:T(8,128)S(1)} %fusion.600), channel_id=1, source_target_pairs={{8,0},{16,8},{24,16},{32,24},{40,32},{48,40},{56,48},{64,56},{72,6... | collective-permute-start | bytes 786440 | tf_op jit(solution)/shard_map/while/body/eval_jaxpr/ppermute | solution.py:10
  465.3 6.5 %collective-permute-done = f32[64,8,128]{2,0,1:T(8,128)S(1)} collective-permute-done((f32[64,8,128]{2,0,1:T(8,128)S(1)}, f32[64,8,128]{2,0,1:T(8,128)S(1)}, u32[]{:S(2)}, u32[]{:S(2)}) %collective-permute-start) | collective-permute-done | bytes 262176 | tf_op jit(solution)/shard_map/while/body/eval_jaxpr/ppermute | solution.py:10
  472.1 6.5 %collective-permute-start = (f32[64,8,128]{2,0,1:T(8,128)S(1)}, f32[64,8,128]{2,0,1:T(8,128)S(1)}, u32[]{:S(2)}, u32[]{:S(2)}) collective-permute-start(f32[64,8,128]{2,0,1:T(8,128)S(1)} %fusion.600), channel_id=1, source_target_pairs={{8,0},{16,8},{24,16},{32,24},{40,32},{48,40},{56,48},{64,56},{72,6... | collective-permute-start | bytes 786440 | tf_op jit(solution)/shard_map/while/body/eval_jaxpr/ppermute | solution.py:10
  478.6 5.6 collective-permute-done
  484.6 6.5 %collective-permute-start = (f32[64,8,128]{2,0,1:T(8,128)S(1)}, f32[64,8,128]{2,0,1:T(8,128)S(1)}, u32[]{:S(2)}, u32[]{:S(2)}) collective-permute-start(f32[64,8,128]{2,0,1:T(8,128)S(1)} %fusion.600), channel_id=1, source_target_pairs={{8,0},{16,8},{24,16},{32,24},{40,32},{48,40},{56,48},{64,56},{72,6... | collective-permute-start | bytes 786440 | tf_op jit(solution)/shard_map/while/body/eval_jaxpr/ppermute | solution.py:10
  491.1 4.8 collective-permute-done
  496.2 6.5 %collective-permute-start = (f32[64,8,128]{2,0,1:T(8,128)S(1)}, f32[64,8,128]{2,0,1:T(8,128)S(1)}, u32[]{:S(2)}, u32[]{:S(2)}) collective-permute-start(f32[64,8,128]{2,0,1:T(8,128)S(1)} %fusion.600), channel_id=1, source_target_pairs={{8,0},{16,8},{24,16},{32,24},{40,32},{48,40},{56,48},{64,56},{72,6... | collective-permute-start | bytes 786440 | tf_op jit(solution)/shard_map/while/body/eval_jaxpr/ppermute | solution.py:10
  506.9 6.5 %collective-permute-start = (f32[64,8,128]{2,0,1:T(8,128)S(1)}, f32[64,8,128]{2,0,1:T(8,128)S(1)}, u32[]{:S(2)}, u32[]{:S(2)}) collective-permute-start(f32[64,8,128]{2,0,1:T(8,128)S(1)} %fusion.600), channel_id=1, source_target_pairs={{8,0},{16,8},{24,16},{32,24},{40,32},{48,40},{56,48},{64,56},{72,6... | collective-permute-start | bytes 786440 | tf_op jit(solution)/shard_map/while/body/eval_jaxpr/ppermute | solution.py:10
  517.7 6.5 %collective-permute-start = (f32[64,8,128]{2,0,1:T(8,128)S(1)}, f32[64,8,128]{2,0,1:T(8,128)S(1)}, u32[]{:S(2)}, u32[]{:S(2)}) collective-permute-start(f32[64,8,128]{2,0,1:T(8,128)S(1)} %fusion.600), channel_id=1, source_target_pairs={{8,0},{16,8},{24,16},{32,24},{40,32},{48,40},{56,48},{64,56},{72,6... | collective-permute-start | bytes 786440 | tf_op jit(solution)/shard_map/while/body/eval_jaxpr/ppermute | solution.py:10
  528.4 6.5 %collective-permute-start = (f32[64,8,128]{2,0,1:T(8,128)S(1)}, f32[64,8,128]{2,0,1:T(8,128)S(1)}, u32[]{:S(2)}, u32[]{:S(2)}) collective-permute-start(f32[64,8,128]{2,0,1:T(8,128)S(1)} %fusion.600), channel_id=1, source_target_pairs={{8,0},{16,8},{24,16},{32,24},{40,32},{48,40},{56,48},{64,56},{72,6... | collective-permute-start | bytes 786440 | tf_op jit(solution)/shard_map/while/body/eval_jaxpr/ppermute | solution.py:10
  539.2 6.5 %collective-permute-start = (f32[64,8,128]{2,0,1:T(8,128)S(1)}, f32[64,8,128]{2,0,1:T(8,128)S(1)}, u32[]{:S(2)}, u32[]{:S(2)}) collective-permute-start(f32[64,8,128]{2,0,1:T(8,128)S(1)} %fusion.600), channel_id=1, source_target_pairs={{8,0},{16,8},{24,16},{32,24},{40,32},{48,40},{56,48},{64,56},{72,6... | collective-permute-start | bytes 786440 | tf_op jit(solution)/shard_map/while/body/eval_jaxpr/ppermute | solution.py:10
  545.7 4.4 collective-permute-done
  550.4 6.5 %collective-permute-start = (f32[64,8,128]{2,0,1:T(8,128)S(1)}, f32[64,8,128]{2,0,1:T(8,128)S(1)}, u32[]{:S(2)}, u32[]{:S(2)}) collective-permute-start(f32[64,8,128]{2,0,1:T(8,128)S(1)} %fusion.600), channel_id=1, source_target_pairs={{8,0},{16,8},{24,16},{32,24},{40,32},{48,40},{56,48},{64,56},{72,6... | collective-permute-start | bytes 786440 | tf_op jit(solution)/shard_map/while/body/eval_jaxpr/ppermute | solution.py:10
  557.0 5.5 collective-permute-done
  562.9 6.5 %collective-permute-start = (f32[64,8,128]{2,0,1:T(8,128)S(1)}, f32[64,8,128]{2,0,1:T(8,128)S(1)}, u32[]{:S(2)}, u32[]{:S(2)}) collective-permute-start(f32[64,8,128]{2,0,1:T(8,128)S(1)} %fusion.600), channel_id=1, source_target_pairs={{8,0},{16,8},{24,16},{32,24},{40,32},{48,40},{56,48},{64,56},{72,6... | collective-permute-start | bytes 786440 | tf_op jit(solution)/shard_map/while/body/eval_jaxpr/ppermute | solution.py:10
  569.4 6.7 %collective-permute-done = f32[64,8,128]{2,0,1:T(8,128)S(1)} collective-permute-done((f32[64,8,128]{2,0,1:T(8,128)S(1)}, f32[64,8,128]{2,0,1:T(8,128)S(1)}, u32[]{:S(2)}, u32[]{:S(2)}) %collective-permute-start) | collective-permute-done | bytes 262176 | tf_op jit(solution)/shard_map/while/body/eval_jaxpr/ppermute | solution.py:10
  576.4 6.5 %collective-permute-start = (f32[64,8,128]{2,0,1:T(8,128)S(1)}, f32[64,8,128]{2,0,1:T(8,128)S(1)}, u32[]{:S(2)}, u32[]{:S(2)}) collective-permute-start(f32[64,8,128]{2,0,1:T(8,128)S(1)} %fusion.600), channel_id=1, source_target_pairs={{8,0},{16,8},{24,16},{32,24},{40,32},{48,40},{56,48},{64,56},{72,6... | collective-permute-start | bytes 786440 | tf_op jit(solution)/shard_map/while/body/eval_jaxpr/ppermute | solution.py:10
  587.1 6.5 %collective-permute-start = (f32[64,8,128]{2,0,1:T(8,128)S(1)}, f32[64,8,128]{2,0,1:T(8,128)S(1)}, u32[]{:S(2)}, u32[]{:S(2)}) collective-permute-start(f32[64,8,128]{2,0,1:T(8,128)S(1)} %fusion.600), channel_id=1, source_target_pairs={{8,0},{16,8},{24,16},{32,24},{40,32},{48,40},{56,48},{64,56},{72,6... | collective-permute-start | bytes 786440 | tf_op jit(solution)/shard_map/while/body/eval_jaxpr/ppermute | solution.py:10
  597.9 6.5 %collective-permute-start = (f32[64,8,128]{2,0,1:T(8,128)S(1)}, f32[64,8,128]{2,0,1:T(8,128)S(1)}, u32[]{:S(2)}, u32[]{:S(2)}) collective-permute-start(f32[64,8,128]{2,0,1:T(8,128)S(1)} %fusion.600), channel_id=1, source_target_pairs={{8,0},{16,8},{24,16},{32,24},{40,32},{48,40},{56,48},{64,56},{72,6... | collective-permute-start | bytes 786440 | tf_op jit(solution)/shard_map/while/body/eval_jaxpr/ppermute | solution.py:10
  (310 shorter events, 247.6 us)
Async XLA Ops:
  1.7 13.5 %collective-permute-start.1 = (f32[64,8,128]{2,0,1:T(8,128)S(1)}, f32[64,8,128]{2,0,1:T(8,128)S(1)}, u32[]{:S(2)}, u32[]{:S(2)}) collective-permute-start(f32[64,8,128]{2,0,1:T(8,128)S(1)} %bitcast.601), channel_id=1, source_target_pairs={{8,0},{16,8},{24,16},{32,24},{40,32},{48,40},{56,48},{64,56},{72,6... | collective-permute-start | bytes 786440 | tf_op jit(solution)/shard_map/ppermute | solution.py:10
  15.2 5.5 collective-permute-start.2
  18.7 5.8 collective-permute-start.3
  31.2 5.1 collective-permute-start.6
  34.6 5.8 collective-permute-start.7
  47.0 4.8 collective-permute-start.10
  50.2 5.8 collective-permute-start.11
  62.6 3.6 collective-permute-start.14
  64.6 5.8 collective-permute-start.15
  77.0 3.6 collective-permute-start.18
  78.9 5.8 collective-permute-start.19
  91.3 4.1 collective-permute-start.22
  93.2 5.8 collective-permute-start.23
  105.7 3.6 collective-permute-start.26
  107.7 5.8 collective-permute-start.27
  120.1 3.6 collective-permute-start.30
  122.0 5.8 collective-permute-start.31
  134.5 3.6 collective-permute-start.34
  136.5 5.8 collective-permute-start.35
  149.0 3.6 collective-permute-start.38
  150.9 5.8 collective-permute-start.39
  163.3 3.6 collective-permute-start.42
  165.2 5.8 collective-permute-start.43
  177.6 3.6 collective-permute-start.46
  179.6 5.8 collective-permute-start.47
  192.1 3.6 collective-permute-start.50
  194.0 5.8 collective-permute-start.51
  206.4 3.6 collective-permute-start.54
  208.3 5.8 collective-permute-start.55
  220.8 3.6 collective-permute-start.58
  222.7 5.8 collective-permute-start.59
  235.2 3.6 collective-permute-start.62
  237.1 5.8 collective-permute-start.63
  251.1 12.5 %collective-permute-start = (f32[64,8,128]{2,0,1:T(8,128)S(1)}, f32[64,8,128]{2,0,1:T(8,128)S(1)}, u32[]{:S(2)}, u32[]{:S(2)}) collective-permute-start(f32[64,8,128]{2,0,1:T(8,128)S(1)} %fusion.600), channel_id=1, source_target_pairs={{8,0},{16,8},{24,16},{32,24},{40,32},{48,40},{56,48},{64,56},{72,6... | collective-permute-start | bytes 786440 | tf_op jit(solution)/shard_map/while/body/eval_jaxpr/ppermute | solution.py:10
  264.0 11.8 %collective-permute-start = (f32[64,8,128]{2,0,1:T(8,128)S(1)}, f32[64,8,128]{2,0,1:T(8,128)S(1)}, u32[]{:S(2)}, u32[]{:S(2)}) collective-permute-start(f32[64,8,128]{2,0,1:T(8,128)S(1)} %fusion.600), channel_id=1, source_target_pairs={{8,0},{16,8},{24,16},{32,24},{40,32},{48,40},{56,48},{64,56},{72,6... | collective-permute-start | bytes 786440 | tf_op jit(solution)/shard_map/while/body/eval_jaxpr/ppermute | solution.py:10
  276.1 10.9 %collective-permute-start = (f32[64,8,128]{2,0,1:T(8,128)S(1)}, f32[64,8,128]{2,0,1:T(8,128)S(1)}, u32[]{:S(2)}, u32[]{:S(2)}) collective-permute-start(f32[64,8,128]{2,0,1:T(8,128)S(1)} %fusion.600), channel_id=1, source_target_pairs={{8,0},{16,8},{24,16},{32,24},{40,32},{48,40},{56,48},{64,56},{72,6... | collective-permute-start | bytes 786440 | tf_op jit(solution)/shard_map/while/body/eval_jaxpr/ppermute | solution.py:10
  287.4 10.4 %collective-permute-start = (f32[64,8,128]{2,0,1:T(8,128)S(1)}, f32[64,8,128]{2,0,1:T(8,128)S(1)}, u32[]{:S(2)}, u32[]{:S(2)}) collective-permute-start(f32[64,8,128]{2,0,1:T(8,128)S(1)} %fusion.600), channel_id=1, source_target_pairs={{8,0},{16,8},{24,16},{32,24},{40,32},{48,40},{56,48},{64,56},{72,6... | collective-permute-start | bytes 786440 | tf_op jit(solution)/shard_map/while/body/eval_jaxpr/ppermute | solution.py:10
  298.1 10.4 %collective-permute-start = (f32[64,8,128]{2,0,1:T(8,128)S(1)}, f32[64,8,128]{2,0,1:T(8,128)S(1)}, u32[]{:S(2)}, u32[]{:S(2)}) collective-permute-start(f32[64,8,128]{2,0,1:T(8,128)S(1)} %fusion.600), channel_id=1, source_target_pairs={{8,0},{16,8},{24,16},{32,24},{40,32},{48,40},{56,48},{64,56},{72,6... | collective-permute-start | bytes 786440 | tf_op jit(solution)/shard_map/while/body/eval_jaxpr/ppermute | solution.py:10
  308.9 10.4 %collective-permute-start = (f32[64,8,128]{2,0,1:T(8,128)S(1)}, f32[64,8,128]{2,0,1:T(8,128)S(1)}, u32[]{:S(2)}, u32[]{:S(2)}) collective-permute-start(f32[64,8,128]{2,0,1:T(8,128)S(1)} %fusion.600), channel_id=1, source_target_pairs={{8,0},{16,8},{24,16},{32,24},{40,32},{48,40},{56,48},{64,56},{72,6... | collective-permute-start | bytes 786440 | tf_op jit(solution)/shard_map/while/body/eval_jaxpr/ppermute | solution.py:10
  319.6 10.4 %collective-permute-start = (f32[64,8,128]{2,0,1:T(8,128)S(1)}, f32[64,8,128]{2,0,1:T(8,128)S(1)}, u32[]{:S(2)}, u32[]{:S(2)}) collective-permute-start(f32[64,8,128]{2,0,1:T(8,128)S(1)} %fusion.600), channel_id=1, source_target_pairs={{8,0},{16,8},{24,16},{32,24},{40,32},{48,40},{56,48},{64,56},{72,6... | collective-permute-start | bytes 786440 | tf_op jit(solution)/shard_map/while/body/eval_jaxpr/ppermute | solution.py:10
  330.3 11.3 %collective-permute-start = (f32[64,8,128]{2,0,1:T(8,128)S(1)}, f32[64,8,128]{2,0,1:T(8,128)S(1)}, u32[]{:S(2)}, u32[]{:S(2)}) collective-permute-start(f32[64,8,128]{2,0,1:T(8,128)S(1)} %fusion.600), channel_id=1, source_target_pairs={{8,0},{16,8},{24,16},{32,24},{40,32},{48,40},{56,48},{64,56},{72,6... | collective-permute-start | bytes 786440 | tf_op jit(solution)/shard_map/while/body/eval_jaxpr/ppermute | solution.py:10
  342.0 12.5 %collective-permute-start = (f32[64,8,128]{2,0,1:T(8,128)S(1)}, f32[64,8,128]{2,0,1:T(8,128)S(1)}, u32[]{:S(2)}, u32[]{:S(2)}) collective-permute-start(f32[64,8,128]{2,0,1:T(8,128)S(1)} %fusion.600), channel_id=1, source_target_pairs={{8,0},{16,8},{24,16},{32,24},{40,32},{48,40},{56,48},{64,56},{72,6... | collective-permute-start | bytes 786440 | tf_op jit(solution)/shard_map/while/body/eval_jaxpr/ppermute | solution.py:10
  354.9 12.7 %collective-permute-start = (f32[64,8,128]{2,0,1:T(8,128)S(1)}, f32[64,8,128]{2,0,1:T(8,128)S(1)}, u32[]{:S(2)}, u32[]{:S(2)}) collective-permute-start(f32[64,8,128]{2,0,1:T(8,128)S(1)} %fusion.600), channel_id=1, source_target_pairs={{8,0},{16,8},{24,16},{32,24},{40,32},{48,40},{56,48},{64,56},{72,6... | collective-permute-start | bytes 786440 | tf_op jit(solution)/shard_map/while/body/eval_jaxpr/ppermute | solution.py:10
  368.0 11.9 %collective-permute-start = (f32[64,8,128]{2,0,1:T(8,128)S(1)}, f32[64,8,128]{2,0,1:T(8,128)S(1)}, u32[]{:S(2)}, u32[]{:S(2)}) collective-permute-start(f32[64,8,128]{2,0,1:T(8,128)S(1)} %fusion.600), channel_id=1, source_target_pairs={{8,0},{16,8},{24,16},{32,24},{40,32},{48,40},{56,48},{64,56},{72,6... | collective-permute-start | bytes 786440 | tf_op jit(solution)/shard_map/while/body/eval_jaxpr/ppermute | solution.py:10
  380.3 11.1 %collective-permute-start = (f32[64,8,128]{2,0,1:T(8,128)S(1)}, f32[64,8,128]{2,0,1:T(8,128)S(1)}, u32[]{:S(2)}, u32[]{:S(2)}) collective-permute-start(f32[64,8,128]{2,0,1:T(8,128)S(1)} %fusion.600), channel_id=1, source_target_pairs={{8,0},{16,8},{24,16},{32,24},{40,32},{48,40},{56,48},{64,56},{72,6... | collective-permute-start | bytes 786440 | tf_op jit(solution)/shard_map/while/body/eval_jaxpr/ppermute | solution.py:10
  391.7 10.4 %collective-permute-start = (f32[64,8,128]{2,0,1:T(8,128)S(1)}, f32[64,8,128]{2,0,1:T(8,128)S(1)}, u32[]{:S(2)}, u32[]{:S(2)}) collective-permute-start(f32[64,8,128]{2,0,1:T(8,128)S(1)} %fusion.600), channel_id=1, source_target_pairs={{8,0},{16,8},{24,16},{32,24},{40,32},{48,40},{56,48},{64,56},{72,6... | collective-permute-start | bytes 786440 | tf_op jit(solution)/shard_map/while/body/eval_jaxpr/ppermute | solution.py:10
  402.4 10.4 %collective-permute-start = (f32[64,8,128]{2,0,1:T(8,128)S(1)}, f32[64,8,128]{2,0,1:T(8,128)S(1)}, u32[]{:S(2)}, u32[]{:S(2)}) collective-permute-start(f32[64,8,128]{2,0,1:T(8,128)S(1)} %fusion.600), channel_id=1, source_target_pairs={{8,0},{16,8},{24,16},{32,24},{40,32},{48,40},{56,48},{64,56},{72,6... | collective-permute-start | bytes 786440 | tf_op jit(solution)/shard_map/while/body/eval_jaxpr/ppermute | solution.py:10
  413.2 10.4 %collective-permute-start = (f32[64,8,128]{2,0,1:T(8,128)S(1)}, f32[64,8,128]{2,0,1:T(8,128)S(1)}, u32[]{:S(2)}, u32[]{:S(2)}) collective-permute-start(f32[64,8,128]{2,0,1:T(8,128)S(1)} %fusion.600), channel_id=1, source_target_pairs={{8,0},{16,8},{24,16},{32,24},{40,32},{48,40},{56,48},{64,56},{72,6... | collective-permute-start | bytes 786440 | tf_op jit(solution)/shard_map/while/body/eval_jaxpr/ppermute | solution.py:10
  423.9 10.4 %collective-permute-start = (f32[64,8,128]{2,0,1:T(8,128)S(1)}, f32[64,8,128]{2,0,1:T(8,128)S(1)}, u32[]{:S(2)}, u32[]{:S(2)}) collective-permute-start(f32[64,8,128]{2,0,1:T(8,128)S(1)} %fusion.600), channel_id=1, source_target_pairs={{8,0},{16,8},{24,16},{32,24},{40,32},{48,40},{56,48},{64,56},{72,6... | collective-permute-start | bytes 786440 | tf_op jit(solution)/shard_map/while/body/eval_jaxpr/ppermute | solution.py:10
  434.7 11.1 %collective-permute-start = (f32[64,8,128]{2,0,1:T(8,128)S(1)}, f32[64,8,128]{2,0,1:T(8,128)S(1)}, u32[]{:S(2)}, u32[]{:S(2)}) collective-permute-start(f32[64,8,128]{2,0,1:T(8,128)S(1)} %fusion.600), channel_id=1, source_target_pairs={{8,0},{16,8},{24,16},{32,24},{40,32},{48,40},{56,48},{64,56},{72,6... | collective-permute-start | bytes 786440 | tf_op jit(solution)/shard_map/while/body/eval_jaxpr/ppermute | solution.py:10
  446.2 12.2 %collective-permute-start = (f32[64,8,128]{2,0,1:T(8,128)S(1)}, f32[64,8,128]{2,0,1:T(8,128)S(1)}, u32[]{:S(2)}, u32[]{:S(2)}) collective-permute-start(f32[64,8,128]{2,0,1:T(8,128)S(1)} %fusion.600), channel_id=1, source_target_pairs={{8,0},{16,8},{24,16},{32,24},{40,32},{48,40},{56,48},{64,56},{72,6... | collective-permute-start | bytes 786440 | tf_op jit(solution)/shard_map/while/body/eval_jaxpr/ppermute | solution.py:10
  458.8 13.0 %collective-permute-start = (f32[64,8,128]{2,0,1:T(8,128)S(1)}, f32[64,8,128]{2,0,1:T(8,128)S(1)}, u32[]{:S(2)}, u32[]{:S(2)}) collective-permute-start(f32[64,8,128]{2,0,1:T(8,128)S(1)} %fusion.600), channel_id=1, source_target_pairs={{8,0},{16,8},{24,16},{32,24},{40,32},{48,40},{56,48},{64,56},{72,6... | collective-permute-start | bytes 786440 | tf_op jit(solution)/shard_map/while/body/eval_jaxpr/ppermute | solution.py:10
  472.1 12.1 %collective-permute-start = (f32[64,8,128]{2,0,1:T(8,128)S(1)}, f32[64,8,128]{2,0,1:T(8,128)S(1)}, u32[]{:S(2)}, u32[]{:S(2)}) collective-permute-start(f32[64,8,128]{2,0,1:T(8,128)S(1)} %fusion.600), channel_id=1, source_target_pairs={{8,0},{16,8},{24,16},{32,24},{40,32},{48,40},{56,48},{64,56},{72,6... | collective-permute-start | bytes 786440 | tf_op jit(solution)/shard_map/while/body/eval_jaxpr/ppermute | solution.py:10
  484.6 11.3 %collective-permute-start = (f32[64,8,128]{2,0,1:T(8,128)S(1)}, f32[64,8,128]{2,0,1:T(8,128)S(1)}, u32[]{:S(2)}, u32[]{:S(2)}) collective-permute-start(f32[64,8,128]{2,0,1:T(8,128)S(1)} %fusion.600), channel_id=1, source_target_pairs={{8,0},{16,8},{24,16},{32,24},{40,32},{48,40},{56,48},{64,56},{72,6... | collective-permute-start | bytes 786440 | tf_op jit(solution)/shard_map/while/body/eval_jaxpr/ppermute | solution.py:10
  496.2 10.4 %collective-permute-start = (f32[64,8,128]{2,0,1:T(8,128)S(1)}, f32[64,8,128]{2,0,1:T(8,128)S(1)}, u32[]{:S(2)}, u32[]{:S(2)}) collective-permute-start(f32[64,8,128]{2,0,1:T(8,128)S(1)} %fusion.600), channel_id=1, source_target_pairs={{8,0},{16,8},{24,16},{32,24},{40,32},{48,40},{56,48},{64,56},{72,6... | collective-permute-start | bytes 786440 | tf_op jit(solution)/shard_map/while/body/eval_jaxpr/ppermute | solution.py:10
  506.9 10.4 %collective-permute-start = (f32[64,8,128]{2,0,1:T(8,128)S(1)}, f32[64,8,128]{2,0,1:T(8,128)S(1)}, u32[]{:S(2)}, u32[]{:S(2)}) collective-permute-start(f32[64,8,128]{2,0,1:T(8,128)S(1)} %fusion.600), channel_id=1, source_target_pairs={{8,0},{16,8},{24,16},{32,24},{40,32},{48,40},{56,48},{64,56},{72,6... | collective-permute-start | bytes 786440 | tf_op jit(solution)/shard_map/while/body/eval_jaxpr/ppermute | solution.py:10
  517.7 10.4 %collective-permute-start = (f32[64,8,128]{2,0,1:T(8,128)S(1)}, f32[64,8,128]{2,0,1:T(8,128)S(1)}, u32[]{:S(2)}, u32[]{:S(2)}) collective-permute-start(f32[64,8,128]{2,0,1:T(8,128)S(1)} %fusion.600), channel_id=1, source_target_pairs={{8,0},{16,8},{24,16},{32,24},{40,32},{48,40},{56,48},{64,56},{72,6... | collective-permute-start | bytes 786440 | tf_op jit(solution)/shard_map/while/body/eval_jaxpr/ppermute | solution.py:10
  528.4 10.4 %collective-permute-start = (f32[64,8,128]{2,0,1:T(8,128)S(1)}, f32[64,8,128]{2,0,1:T(8,128)S(1)}, u32[]{:S(2)}, u32[]{:S(2)}) collective-permute-start(f32[64,8,128]{2,0,1:T(8,128)S(1)} %fusion.600), channel_id=1, source_target_pairs={{8,0},{16,8},{24,16},{32,24},{40,32},{48,40},{56,48},{64,56},{72,6... | collective-permute-start | bytes 786440 | tf_op jit(solution)/shard_map/while/body/eval_jaxpr/ppermute | solution.py:10
  539.2 10.9 %collective-permute-start = (f32[64,8,128]{2,0,1:T(8,128)S(1)}, f32[64,8,128]{2,0,1:T(8,128)S(1)}, u32[]{:S(2)}, u32[]{:S(2)}) collective-permute-start(f32[64,8,128]{2,0,1:T(8,128)S(1)} %fusion.600), channel_id=1, source_target_pairs={{8,0},{16,8},{24,16},{32,24},{40,32},{48,40},{56,48},{64,56},{72,6... | collective-permute-start | bytes 786440 | tf_op jit(solution)/shard_map/while/body/eval_jaxpr/ppermute | solution.py:10
  550.4 12.0 %collective-permute-start = (f32[64,8,128]{2,0,1:T(8,128)S(1)}, f32[64,8,128]{2,0,1:T(8,128)S(1)}, u32[]{:S(2)}, u32[]{:S(2)}) collective-permute-start(f32[64,8,128]{2,0,1:T(8,128)S(1)} %fusion.600), channel_id=1, source_target_pairs={{8,0},{16,8},{24,16},{32,24},{40,32},{48,40},{56,48},{64,56},{72,6... | collective-permute-start | bytes 786440 | tf_op jit(solution)/shard_map/while/body/eval_jaxpr/ppermute | solution.py:10
  562.9 13.2 %collective-permute-start = (f32[64,8,128]{2,0,1:T(8,128)S(1)}, f32[64,8,128]{2,0,1:T(8,128)S(1)}, u32[]{:S(2)}, u32[]{:S(2)}) collective-permute-start(f32[64,8,128]{2,0,1:T(8,128)S(1)} %fusion.600), channel_id=1, source_target_pairs={{8,0},{16,8},{24,16},{32,24},{40,32},{48,40},{56,48},{64,56},{72,6... | collective-permute-start | bytes 786440 | tf_op jit(solution)/shard_map/while/body/eval_jaxpr/ppermute | solution.py:10
  576.4 10.4 %collective-permute-start = (f32[64,8,128]{2,0,1:T(8,128)S(1)}, f32[64,8,128]{2,0,1:T(8,128)S(1)}, u32[]{:S(2)}, u32[]{:S(2)}) collective-permute-start(f32[64,8,128]{2,0,1:T(8,128)S(1)} %fusion.600), channel_id=1, source_target_pairs={{8,0},{16,8},{24,16},{32,24},{40,32},{48,40},{56,48},{64,56},{72,6... | collective-permute-start | bytes 786440 | tf_op jit(solution)/shard_map/while/body/eval_jaxpr/ppermute | solution.py:10
  587.1 10.4 %collective-permute-start = (f32[64,8,128]{2,0,1:T(8,128)S(1)}, f32[64,8,128]{2,0,1:T(8,128)S(1)}, u32[]{:S(2)}, u32[]{:S(2)}) collective-permute-start(f32[64,8,128]{2,0,1:T(8,128)S(1)} %fusion.600), channel_id=1, source_target_pairs={{8,0},{16,8},{24,16},{32,24},{40,32},{48,40},{56,48},{64,56},{72,6... | collective-permute-start | bytes 786440 | tf_op jit(solution)/shard_map/while/body/eval_jaxpr/ppermute | solution.py:10
  597.9 10.4 %collective-permute-start = (f32[64,8,128]{2,0,1:T(8,128)S(1)}, f32[64,8,128]{2,0,1:T(8,128)S(1)}, u32[]{:S(2)}, u32[]{:S(2)}) collective-permute-start(f32[64,8,128]{2,0,1:T(8,128)S(1)} %fusion.600), channel_id=1, source_target_pairs={{8,0},{16,8},{24,16},{32,24},{40,32},{48,40},{56,48},{64,56},{72,6... | collective-permute-start | bytes 786440 | tf_op jit(solution)/shard_map/while/body/eval_jaxpr/ppermute | solution.py:10
  (39 other events, 155.3 us)
where the time goes:
time: 620 us; the launch traced here: 610 us
  starting transfers between devices  307 us (50%)
  waiting for transfers between devices  236 us (38%)
  matrix products  56.5 us (9%)
  local copies, waits for them, and re-layouts  6.2 us (1%)
    ppermute x32, starting transfers between devices, passed_along(): lax.ppermute(value, axis, [(source, source + steps) for source in range(i...  209 us
    ppermute x32, waiting for transfers between devices, passed_along(): lax.ppermute(value, axis, [(source, source + steps) for source in range(i...  150 us
    ppermute x32, waiting for transfers between devices, padded_2(): lax.ppermute(head, axis, [((i + 1) % count, i) for i in range(ends)])  86 us
    ppermute x32, starting transfers between devices, padded_2(): lax.ppermute(tail, axis, [(i, (i + 1) % count) for i in range(ends)])  56 us
    dot_general x80, matrix products, batched(): jnp.einsum('ij,cjxy->cixy', matrix, field, precision=lax.Precision.HIGHEST)  44.7 us
    ppermute x32, starting transfers between devices, padded_2(): lax.ppermute(head, axis, [((i + 1) % count, i) for i in range(ends)])  42.2 us
  transfers between devices with their start and end apart: 96, of which 64 were waited for; matrix products, arithmetic and copies ran while one was open for 3% of the time, Pallas kernels for 0%

commit v1 on v0

v1 whole, which is shorter than its diff:
```python
import functools

import jax
import jax.numpy as jnp
from jax import lax
from jax.experimental import pallas as pl
from jax.experimental.pallas import tpu as pltpu
from jax.sharding import PartitionSpec as P

MESH = pl.DeviceIdType.MESH
F32, BF16 = jnp.float32, jnp.bfloat16

NT, NZ, NY, NX = 32, 8, 4, 4
DOF, STEPS, LANES = 64, 16, 128
STRIP, HALO = 32, 16


def split(value):
    high = value.astype(BF16)
    return high, (value - high.astype(F32)).astype(BF16)


def right_operand(value):
    high, low = split(value)
    return jnp.concatenate([high, low, high, low], axis=0)


def left_operand(ref, rows, value, temporary):
    high = value.astype(BF16).astype(F32)
    low = value - high
    size = value.shape[0]
    for slot, part in enumerate((high, high, low, low)):
        temporary[0:size, 64 * slot : 64 * slot + 64] = part
    ref[rows, :] = temporary[0:size, :].astype(BF16)


def mul(left, right):
    return jnp.dot(left, right, preferred_element_type=F32)


def exact(left, right):
    return jnp.dot(left, right, precision=lax.Precision.HIGHEST, preferred_element_type=F32)


def kernel(
    g_hbm, f_hbm, weight, mask_hbm, fine, coupling, coarse,
    upd_hbm, res_hbm,
    gv, fv, g_edge, f_edge, mask_in, g_pack, f_pack, start, strip_f, strip_g, mask_s,
    fine_op, temporary, powers, power_op, state, product, last, dense, gathered, scan, total, totals,
    e_out, res_parts, e_parts, upd_v, res_v,
    load_sem, store_sem, edge_send, edge_recv, start_send, start_recv, f_send, f_recv, g_send, g_recv,
    d_send, d_recv, r_send, r_recv, t_send, t_recv, e_send, e_recv,
):
    tm, gx, gy = lax.axis_index("tm"), lax.axis_index("gx"), lax.axis_index("gy")
    y, z = tm // NZ, lax.rem(tm, NZ)
    owner = z // 2
    returns_here = owner == gx
    lane = lax.broadcasted_iota(jnp.int32, (64, LANES), 1)
    lane8 = lax.broadcasted_iota(jnp.int32, (8, LANES), 1)

    def remote(source, target, send, recv, device):
        return pltpu.make_async_remote_copy(
            src_ref=source, dst_ref=target, send_sem=send, recv_sem=recv, device_id=device, device_id_type=MESH
        )

    g_load = pltpu.make_async_copy(g_hbm, gv, load_sem.at[0])
    f_load = pltpu.make_async_copy(f_hbm, fv.at[pl.ds(0, 512)], load_sem.at[1])
    m_load = pltpu.make_async_copy(mask_hbm, mask_in, load_sem.at[2])
    g_load.start()
    m_load.start()
    f_load.start()

    barrier = pltpu.get_barrier_semaphore()

    def tell(device):
        pl.semaphore_signal(barrier, inc=1, device_id=device, device_id_type=MESH)

    later = lax.rem(tm + 1, NT)
    earlier = lax.rem(tm + NT - 1, NT)
    tell((tm, gx, 1 - gy))
    for q in range(NX):
        tell((later, q, gy))
    for d in range(1, NX):
        tell((tm, lax.rem(gx + d, NX), gy))
    for d in range(1, NZ):
        tell((y * NZ + lax.rem(z + d, NZ), gx, gy))
    for d in range(1, NY):
        tell((lax.rem(y + d, NY) * NZ + z, gx, gy))
    for h in range(2):
        for q in range(NX):
            @pl.when(jnp.logical_not(jnp.logical_and(2 * gx + h == z, gx == q)))
            def _():
                tell((y * NZ + 2 * gx + h, q, gy))

    m_load.wait()
    fv[512:520, :] = mask_in[...].astype(F32)
    g_load.wait()
    f_load.wait()

    def window(low_row, high_row, q):
        begin = STRIP * q - HALO
        where = lane[: low_row.shape[0]]
        return jnp.where(
            where < 64, pltpu.roll(low_row, (-begin) % LANES, 1), pltpu.roll(high_row, (64 - begin) % LANES, 1)
        )

    has_low = (gy == 1).astype(F32)
    has_high = (gy == 0).astype(F32)

    def extended(own, edge, q):
        where = lane[: own.shape[0]]
        if q == 0:
            return jnp.where(where >= LANES - HALO, edge * has_low, own)
        if q == NX - 1:
            return jnp.where(where < HALO, edge * has_high, own)
        return own

    def row(ref, x):
        return ref[pl.ds(x, DOF, stride=8), :]

    def pack(own, edge, out, q):
        for i in range(4):
            parts = []
            for x in (i, i + 4):
                mine = row(own, x)
                parts.append(extended(mine, row(edge, x), q) if q in (0, NX - 1) else mine)
            out[q, 64 * i : 64 * i + 64, :] = window(parts[0], parts[1], q)

    def pack_mask(q):
        mine = fv[512:520, :]
        if q in (0, NX - 1):
            mine = extended(mine, f_edge[512:520, :], q)
        f_pack[q, 256:264, :] = window(mine, pltpu.roll(mine, 4, 0), q)

    g_swap = remote(gv, g_edge, edge_send.at[0], edge_recv.at[0], (tm, gx, 1 - gy))
    f_swap = remote(fv, f_edge, edge_send.at[1], edge_recv.at[1], (tm, gx, 1 - gy))

    def start_copy(q):
        return remote(g_pack.at[q], start.at[gx], start_send.at[q], start_recv.at[gx], (earlier, q, gy))

    def strip_copy(source, target, send, recv, q):
        return remote(source.at[q], target.at[gx], send.at[q], recv.at[gx], (tm, q, gy))

    def strip_send(source, target, send, recv, q):
        @pl.when(gx != q)
        def _():
            strip_copy(source, target, send, recv, q).start()

        @pl.when(gx == q)
        def _():
            pltpu.make_async_copy(source.at[q], target.at[gx], recv.at[gx]).start()

    for q in (1, 2):
        pack(gv, None, g_pack, q)
    pl.semaphore_wait(barrier, 26 - returns_here.astype(jnp.int32))
    g_swap.start()
    f_swap.start()
    for q in (1, 2):
        start_copy(q).start()
    for q in (1, 2):
        pack(fv, None, f_pack, q)
        pack_mask(q)
        strip_send(f_pack, strip_f, f_send, f_recv, q)
    g_swap.wait_recv()
    for q in (0, 3):
        pack(gv, g_edge, g_pack, q)
        start_copy(q).start()
    f_swap.wait_recv()
    for q in (0, 3):
        pack(fv, f_edge, f_pack, q)
        pack_mask(q)
        strip_send(f_pack, strip_f, f_send, f_recv, q)
    for q in range(NX):
        strip_send(g_pack, strip_g, g_send, g_recv, q)

    left_operand(fine_op, pl.ds(0, 64), fine[...], temporary)
    left_operand(fine_op, pl.ds(64, 256), coupling[...], temporary)
    c1 = coarse[...]
    powers[0:64, :] = c1
    c2 = exact(c1, c1)
    powers[64:128, :] = c2
    powers[128:256, :] = exact(powers[0:128, :], c2)
    powers[256:512, :] = exact(powers[0:256, :], powers[192:256, :])
    c8 = powers[448:512, :]
    c16 = exact(c8, c8)
    left_operand(power_op, pl.ds(0, 512), powers[...], temporary)
    left_operand(power_op, pl.ds(512, 64), c16, temporary)

    is_last_interval = tm == NT - 1
    for q in range(NX):
        remote(g_pack.at[q], start.at[q], start_send.at[q], start_recv.at[q], (earlier, q, gy)).wait_recv()
        for i in range(4):
            begin = jnp.where(is_last_interval, 0.0, start[q, 64 * i : 64 * i + 64, :])
            high, low = split(begin)
            pair, half = 2 * q + i // 2, LANES * (i % 2)
            state[pair, 0:64, half : half + LANES] = high
            state[pair, 64:128, half : half + LANES] = low
    for q in range(NX):
        remote(f_pack.at[q], strip_f.at[q], f_send.at[q], f_recv.at[q], (tm, q, gy)).wait_recv()
        for i in range(4):
            mask_s[4 * q + i] = jnp.broadcast_to(strip_f[q, 256 + i : 257 + i, :], (8, LANES))

    def part(q, i, kind):
        half = LANES * (i % 2)
        return product[2 * q + i // 2, 64 * kind : 64 * kind + 64, half : half + LANES]

    def fine_step(k, final):
        for pair in range(8):
            rows = state[pair]
            product[pair] = mul(fine_op[...], jnp.concatenate([rows, rows], axis=0))
        scale = weight[k]
        low_half = lane < 64
        for q in range(NX):
            for i in range(4):
                if i > 0:
                    west = part(q, i - 1, 1)
                else:
                    before = part(q - 1, 3, 1) if q > 0 else jnp.zeros((64, LANES), F32)
                    west = pltpu.roll(jnp.where(low_half, part(q, 3, 1), before), 64, 1)
                if i < 3:
                    east = part(q, i + 1, 2)
                else:
                    after = part(q + 1, 0, 2) if q < NX - 1 else jnp.zeros((64, LANES), F32)
                    east = pltpu.roll(jnp.where(low_half, after, part(q, 0, 2)), 64, 1)
                south = pltpu.roll(part(q, i, 3), 1, 1)
                north = pltpu.roll(part(q, i, 4), LANES - 1, 1)
                value = (part(q, i, 0) + west) + (east + south) + (north + scale * strip_f[q, 64 * i : 64 * i + 64, :])
                mask = mask_s[4 * q + i]
                value = (value.reshape(8, 8, LANES) * mask[None]).reshape(64, LANES)
                if final:
                    last[4 * q + i] = value
                else:
                    high, low = split(value)
                    pair, half = 2 * q + i // 2, LANES * (i % 2)
                    state[pair, 0:64, half : half + LANES] = high
                    state[pair, 64:128, half : half + LANES] = low

    def body(step, carry):
        fine_step(STEPS - 1 - step, False)
        return carry

    lax.fori_loop(0, STEPS - 1, body, 0)
    fine_step(0, True)

    even_block = lax.rem(lane // STRIP, 2) == 0
    for q in range(NX):
        remote(g_pack.at[q], strip_g.at[q], g_send.at[q], g_recv.at[q], (tm, q, gy)).wait_recv()
        for h in range(2):
            pieces = []
            for i in (2 * h, 2 * h + 1):
                guess = strip_g[q, 64 * i : 64 * i + 64, :].reshape(8, 8, LANES) * mask_s[4 * q + i][None]
                pieces.append(last[4 * q + i] - guess.reshape(64, LANES))
            dense[2 * q + h] = jnp.where(
                even_block, pltpu.roll(pieces[0], LANES - HALO, 1), pltpu.roll(pieces[1], HALO, 1)
            )

    def dense_copy(k):
        return remote(dense.at[k], gathered.at[z], d_send.at[k], d_recv.at[z], (y * NZ + k, gx, gy))

    for k in range(NZ):
        @pl.when(z != k)
        def _():
            dense_copy(k).start()

        @pl.when(z == k)
        def _():
            pltpu.make_async_copy(dense.at[k], gathered.at[z], d_recv.at[z]).start()

    def residual_copy(q):
        return remote(dense.at[pl.ds(2 * q, 2)], res_parts.at[gx], r_send.at[q], r_recv.at[gx], (tm, q, gy))

    for q in range(NX):
        @pl.when(gx != q)
        def _():
            residual_copy(q).start()

        @pl.when(gx == q)
        def _():
            pltpu.make_async_copy(dense.at[pl.ds(2 * q, 2)], res_parts.at[gx], r_recv.at[gx]).start()

    for k in range(NZ):
        remote(dense.at[k], gathered.at[k], d_send.at[k], d_recv.at[k], (y * NZ + k, gx, gy)).wait_recv()
        scan[k] = gathered[k]
        if k > 0:
            terms = mul(power_op[0 : 64 * k, :], right_operand(gathered[k]))
            for p in range(1, k + 1):
                scan[k - p] += terms[64 * (p - 1) : 64 * p, :]
    total[...] = scan[0]

    def total_copy(d):
        return remote(total, totals.at[d - 1], t_send.at[d - 1], t_recv.at[d - 1], (lax.rem(y + NY - d, NY) * NZ + z, gx, gy))

    for d in range(1, NY):
        total_copy(d).start()

    def spread(parts, out, base):
        low_half = lane < 64
        for h in range(2):
            t = [parts[q, h] for q in range(NX)]
            a = [
                jnp.where(low_half, t[0], pltpu.roll(t[2], 64, 1)),
                jnp.where(low_half, t[1], pltpu.roll(t[3], 64, 1)),
                jnp.where(low_half, pltpu.roll(t[0], 64, 1), t[2]),
                jnp.where(low_half, pltpu.roll(t[1], 64, 1), t[3]),
            ]
            for m in range(2):
                first, second = a[2 * m], a[2 * m + 1]
                rows = (
                    jnp.where(even_block, first, pltpu.roll(second, STRIP, 1)),
                    jnp.where(even_block, pltpu.roll(first, LANES - STRIP, 1), second),
                )
                for n in range(2):
                    x = 2 * h + 4 * m + n
                    value = rows[n] if base is None else rows[n] + row(base, x)
                    out[pl.ds(x, DOF, stride=8), :] = value

    for q in range(NX):
        remote(dense.at[pl.ds(2 * q, 2)], res_parts.at[q], r_send.at[q], r_recv.at[q], (tm, q, gy)).wait_recv()
    spread(res_parts, res_v, None)
    res_store = pltpu.make_async_copy(res_v, res_hbm, store_sem.at[0])
    res_store.start()

    for d in range(1, NY):
        total_copy(d).wait_recv()
    zero = jnp.zeros((64, LANES), F32)
    groups = [jnp.where(y + d < NY, totals[d - 1], zero) for d in range(1, NY)]
    entering = groups[0] + mul(power_op[448:512, :], right_operand(groups[1])) + mul(
        power_op[512:576, :], right_operand(groups[2])
    )
    carried = mul(power_op[0:512, :], right_operand(entering))

    def e_copy(k):
        slot = 2 * gx + lax.rem(z, 2)
        return remote(e_out.at[k], e_parts.at[slot], e_send.at[k], e_recv.at[slot], (y * NZ + k, owner, gy))

    for k in range(NZ):
        e_out[k] = scan[k] + carried[64 * (NZ - 1 - k) : 64 * (NZ - k), :]
        here = jnp.logical_and(returns_here, z == k)

        @pl.when(jnp.logical_not(here))
        def _():
            e_copy(k).start()

        @pl.when(here)
        def _():
            slot = 2 * gx + lax.rem(z, 2)
            pltpu.make_async_copy(e_out.at[k], e_parts.at[slot], e_recv.at[slot]).start()

    for slot in range(8):
        remote(e_out.at[0], e_parts.at[slot], e_send.at[0], e_recv.at[slot], (y * NZ, owner, gy)).wait_recv()

    class Tiles:
        def __getitem__(self, index):
            return e_parts[2 * index[0] + index[1]]

    spread(Tiles(), upd_v, gv)
    upd_store = pltpu.make_async_copy(upd_v, upd_hbm, store_sem.at[1])
    upd_store.start()

    g_swap.wait_send()
    f_swap.wait_send()
    for q in range(NX):
        start_copy(q).wait_send()

        @pl.when(gx != q)
        def _():
            strip_copy(f_pack, strip_f, f_send, f_recv, q).wait_send()
            strip_copy(g_pack, strip_g, g_send, g_recv, q).wait_send()
            residual_copy(q).wait_send()

    for k in range(NZ):
        @pl.when(z != k)
        def _():
            dense_copy(k).wait_send()

        @pl.when(jnp.logical_not(jnp.logical_and(returns_here, z == k)))
        def _():
            e_copy(k).wait_send()

    for d in range(1, NY):
        total_copy(d).wait_send()
    res_store.wait()
    upd_store.wait()


def per_device(guesses, forcing, step_weight, land_mask, fine_matrix, coupling, coarse_matrix):
    vmem = pl.BlockSpec(memory_space=pltpu.VMEM)
    anywhere = pl.BlockSpec(memory_space=pl.ANY)
    flat = jax.ShapeDtypeStruct((DOF * 8, LANES), F32)
    dma = pltpu.SemaphoreType.DMA
    updated, residual = pl.pallas_call(
        kernel,
        out_shape=(flat, flat),
        in_specs=[anywhere, anywhere, pl.BlockSpec(memory_space=pltpu.SMEM), anywhere, vmem, vmem, vmem],
        out_specs=(anywhere, anywhere),
        scratch_shapes=[
            pltpu.VMEM((512, LANES), F32),
            pltpu.VMEM((520, LANES), F32),
            pltpu.VMEM((512, LANES), F32),
            pltpu.VMEM((520, LANES), F32),
            pltpu.VMEM((8, LANES), jnp.int32),
            pltpu.VMEM((NX, 256, LANES), F32),
            pltpu.VMEM((NX, 264, LANES), F32),
            pltpu.VMEM((NX, 256, LANES), F32),
            pltpu.VMEM((NX, 264, LANES), F32),
            pltpu.VMEM((NX, 256, LANES), F32),
            pltpu.VMEM((16, 8, LANES), F32),
            pltpu.VMEM((320, 256), BF16),
            pltpu.VMEM((512, 256), F32),
            pltpu.VMEM((512, DOF), F32),
            pltpu.VMEM((576, 256), BF16),
            pltpu.VMEM((8, 128, 256), BF16),
            pltpu.VMEM((8, 320, 256), F32),
            pltpu.VMEM((16, 64, LANES), F32),
            pltpu.VMEM((NZ, 64, LANES), F32),
            pltpu.VMEM((NZ, 64, LANES), F32),
            pltpu.VMEM((NZ, 64, LANES), F32),
            pltpu.VMEM((64, LANES), F32),
            pltpu.VMEM((NY - 1, 64, LANES), F32),
            pltpu.VMEM((NZ, 64, LANES), F32),
            pltpu.VMEM((NX, 2, 64, LANES), F32),
            pltpu.VMEM((8, 64, LANES), F32),
            pltpu.VMEM((512, LANES), F32),
            pltpu.VMEM((512, LANES), F32),
            dma((3,)), dma((2,)), dma((2,)), dma((2,)),
            dma((NX,)), dma((NX,)), dma((NX,)), dma((NX,)), dma((NX,)), dma((NX,)),
            dma((NZ,)), dma((NZ,)), dma((NX,)), dma((NX,)), dma((NY - 1,)), dma((NY - 1,)), dma((NZ,)), dma((8,)),
        ],
        compiler_params=pltpu.CompilerParams(
            collective_id=0, has_side_effects=True, vmem_limit_bytes=24 * 1024 * 1024
        ),
    )(
        guesses.reshape(DOF * 8, LANES), forcing.reshape(DOF * 8, LANES), step_weight, land_mask,
        fine_matrix, coupling.reshape(4 * DOF, DOF), coarse_matrix,
    )
    return updated.reshape(guesses.shape), residual.reshape(guesses.shape)


def solution(mesh):
    tiles = P("tm", None, "gx", "gy")
    return jax.shard_map(
        per_device,
        mesh=mesh,
        in_specs=(tiles, tiles, P(), P("gx", "gy"), P(), P(), P()),
        out_specs=(tiles, tiles),
        check_vma=False,
    )
```

time: 620 us -> 66.8 us (0.11)
  the two profiles are of different devices: /device:TPU:24 before, /device:TPU:2 now
where the time goes in v1:
time: 66.8 us; the launch traced here: 66.1 us
  Pallas kernels  59 us (88%)
  local copies, waits for them, and re-layouts  6.4 us (10%)
    pallas_call x1, Pallas kernels, per_device(): pl.pallas_call(kernel, out_shape=(flat, flat), in_specs=[anywhere, anywhe...  59 us
    unnamed x16, local copies, waits for them, and re-layouts  6.4 us

profile of v1, /device:TPU:2, one launch (start us, length us, event | category | flops | bytes accessed | tf_op | source)
XLA Modules:
  0.0 66.1 jit_solution(13623107005378182159)
XLA Ops:
  0.6 0.0 copy-start.5
  0.6 0.0 copy-start.6
  0.7 0.7 %copy-done.5 = s32[8,128]{1,0:T(8,128)S(1)} copy-done((s32[8,128]{1,0:T(8,128)S(1)}, s32[8,128]{1,0:T(8,128)}, u32[]{:S(2)}) %copy-start.5) | copy-done | bytes 4120
  1.3 0.0 copy-done.6
  1.3 0.0 copy-start
  1.3 0.9 %copy-done = f32[1,64,8,128]{3,2,1,0:T(8,128)S(1)} copy-done((f32[1,64,8,128]{3,2,1,0:T(8,128)S(1)}, f32[1,64,8,128]{3,2,1,0:T(8,128)}, u32[]{:S(2)}) %copy-start) | copy-done | bytes 262168
  2.3 0.0 copy-start.1
  2.3 0.9 %copy-done.1 = f32[1,64,8,128]{3,2,1,0:T(8,128)S(1)} copy-done((f32[1,64,8,128]{3,2,1,0:T(8,128)S(1)}, f32[1,64,8,128]{3,2,1,0:T(8,128)}, u32[]{:S(2)}) %copy-start.1) | copy-done | bytes 262168
  3.2 0.0 copy-start.2
  3.2 0.9 %copy-done.2 = f32[4,64,64]{2,1,0:T(8,128)S(1)} copy-done((f32[4,64,64]{2,1,0:T(8,128)S(1)}, f32[4,64,64]{2,1,0:T(8,128)}, u32[]{:S(2)}) %copy-start.2) | copy-done | bytes 65560
  4.1 0.0 copy-start.3
  4.1 0.8 %copy-done.3 = f32[64,64]{1,0:T(8,128)S(1)} copy-done((f32[64,64]{1,0:T(8,128)S(1)}, f32[64,64]{1,0:T(8,128)}, u32[]{:S(2)}) %copy-start.3) | copy-done | bytes 16408
  4.9 0.0 copy-start.4
  4.9 0.8 %copy-done.4 = f32[64,64]{1,0:T(8,128)S(1)} copy-done((f32[64,64]{1,0:T(8,128)S(1)}, f32[64,64]{1,0:T(8,128)}, u32[]{:S(2)}) %copy-start.4) | copy-done | bytes 16408
  5.6 59.0 %shard_map.86 = (f32[512,128]{1,0:T(8,128)S(1)}, f32[512,128]{1,0:T(8,128)S(1)}) custom-call(f32[512,128]{1,0:T(8,128)S(1)} %bitcast.5, f32[512,128]{1,0:T(8,128)S(1)} %bitcast.6, f32[16]{0:T(128)S(1)} %copy-done.6, s32[8,128]{1,0:T(8,128)S(1)} %copy-done.5, f32[64,64]{1,0:T(8,128)S(1)} %copy-done.3, f32[256,64]{1,0:T(8,128)S(1)} %bitcast.9, ...), custom_call_target="tpu_custom_call" | custom-call | tf_op jit(solution)/shard_map/pallas_call | solution.py:391
  64.7 0.7 %copy.11 = f32[1,64,8,128]{3,2,1,0:T(8,128)} copy(f32[1,64,8,128]{3,2,1,0:T(8,128)S(1)} %bitcast.8) | data formatting | bytes 524288
  65.4 0.7 %copy.12 = f32[1,64,8,128]{3,2,1,0:T(8,128)} copy(f32[1,64,8,128]{3,2,1,0:T(8,128)S(1)} %bitcast.7) | data formatting | bytes 524288
Async XLA Ops:
  0.6 0.7 %copy-start.5 = (s32[8,128]{1,0:T(8,128)S(1)}, s32[8,128]{1,0:T(8,128)}, u32[]{:S(2)}) copy-start(s32[8,128]{1,0:T(8,128)} %mask_hbm.1) | copy-start | bytes 12292
  0.6 0.7 %copy-start.6 = (f32[16]{0:T(128)S(1)}, f32[16]{0:T(128)}, u32[]{:S(2)}) copy-start(f32[16]{0:T(128)} %weight.1) | copy-start | bytes 196
  1.3 1.0 %copy-start = (f32[1,64,8,128]{3,2,1,0:T(8,128)S(1)}, f32[1,64,8,128]{3,2,1,0:T(8,128)}, u32[]{:S(2)}) copy-start(f32[1,64,8,128]{3,2,1,0:T(8,128)} %param.7) | copy-start | bytes 786436
  2.3 0.9 %copy-start.1 = (f32[1,64,8,128]{3,2,1,0:T(8,128)S(1)}, f32[1,64,8,128]{3,2,1,0:T(8,128)}, u32[]{:S(2)}) copy-start(f32[1,64,8,128]{3,2,1,0:T(8,128)} %param.8) | copy-start | bytes 786436
  3.2 0.9 %copy-start.2 = (f32[4,64,64]{2,1,0:T(8,128)S(1)}, f32[4,64,64]{2,1,0:T(8,128)}, u32[]{:S(2)}) copy-start(f32[4,64,64]{2,1,0:T(8,128)} %param.12) | copy-start | bytes 196612
  4.1 0.8 %copy-start.3 = (f32[64,64]{1,0:T(8,128)S(1)}, f32[64,64]{1,0:T(8,128)}, u32[]{:S(2)}) copy-start(f32[64,64]{1,0:T(8,128)} %fine.1) | copy-start | bytes 49156
  4.9 0.8 %copy-start.4 = (f32[64,64]{1,0:T(8,128)S(1)}, f32[64,64]{1,0:T(8,128)}, u32[]{:S(2)}) copy-start(f32[64,64]{1,0:T(8,128)} %coarse.1) | copy-start | bytes 49156

commit v2 on v1

v2 whole, which is shorter than its diff:
```python
import functools

import jax
import jax.numpy as jnp
from jax import lax
from jax.experimental import pallas as pl
from jax.experimental.pallas import tpu as pltpu
from jax.sharding import PartitionSpec as P

MESH = pl.DeviceIdType.MESH
F32, BF16 = jnp.float32, jnp.bfloat16

NT, NZ, NY, NX = 32, 8, 4, 4
DOF, STEPS, LANES = 64, 16, 128
STRIP, HALO = 32, 16


def split(value):
    high = value.astype(BF16)
    return high, (value - high.astype(F32)).astype(BF16)


def right_operand(value):
    high, low = split(value)
    return jnp.concatenate([high, low, high, low], axis=0)


def left_operand(ref, rows, value, temporary):
    high = value.astype(BF16).astype(F32)
    low = value - high
    size = value.shape[0]
    for slot, part in enumerate((high, high, low, low)):
        temporary[0:size, 64 * slot : 64 * slot + 64] = part
    ref[rows, :] = temporary[0:size, :].astype(BF16)


def mul(left, right):
    return jnp.dot(left, right, preferred_element_type=F32)


def exact(left, right):
    return jnp.dot(left, right, precision=lax.Precision.HIGHEST, preferred_element_type=F32)


def kernel(
    g_hbm, f_hbm, weight, mask_hbm, fine_hbm, coupling_hbm, coarse_hbm,
    upd_v, res_v,
    gv, fv, g_edge, f_edge, mask_in, g_pack, f_pack, start, strip_f, strip_g, mask_s, g_dense,
    fine_op, temporary, powers, power_op, state, product, last, dense, packed, gathered, scan, sums,
    e_out, res_parts, e_parts,
    fine, coupling, coarse, load_sem, edge_send, edge_recv, start_send, start_recv, f_send, f_recv, g_send, g_recv,
    d_send, d_recv, r_send, r_recv, e_send, e_recv, group_sem,
):
    tm, gx, gy = lax.axis_index("tm"), lax.axis_index("gx"), lax.axis_index("gy")
    y, z = tm // NZ, lax.rem(tm, NZ)
    owner = z // 2
    returns_here = owner == gx
    lane = lax.broadcasted_iota(jnp.int32, (64, LANES), 1)
    lane8 = lax.broadcasted_iota(jnp.int32, (8, LANES), 1)

    def remote(source, target, send, recv, device):
        return pltpu.make_async_remote_copy(
            src_ref=source, dst_ref=target, send_sem=send, recv_sem=recv, device_id=device, device_id_type=MESH
        )

    g_load = pltpu.make_async_copy(g_hbm, gv, load_sem.at[0])
    f_load = pltpu.make_async_copy(f_hbm, fv.at[pl.ds(0, 512)], load_sem.at[1])
    m_load = pltpu.make_async_copy(mask_hbm, mask_in, load_sem.at[2])
    g_load.start()
    m_load.start()
    f_load.start()
    matrix_loads = [
        pltpu.make_async_copy(source, target, load_sem.at[3 + n])
        for n, (source, target) in enumerate(((fine_hbm, fine), (coupling_hbm, coupling), (coarse_hbm, coarse)))
    ]
    for load in matrix_loads:
        load.start()

    barrier = pltpu.get_barrier_semaphore()

    def tell(device):
        pl.semaphore_signal(barrier, inc=1, device_id=device, device_id_type=MESH)

    later = lax.rem(tm + 1, NT)
    earlier = lax.rem(tm + NT - 1, NT)
    tell((tm, gx, 1 - gy))
    for q in range(NX):
        tell((later, q, gy))
    for d in range(1, NX):
        tell((tm, lax.rem(gx + d, NX), gy))
    for d in range(1, NZ):
        tell((y * NZ + lax.rem(z + d, NZ), gx, gy))
    for d in range(1, NY):
        tell((lax.rem(y + d, NY) * NZ + z, gx, gy))

    m_load.wait()
    fv[512:520, :] = mask_in[...].astype(F32)
    g_load.wait()
    f_load.wait()

    def window(low_row, high_row, q):
        begin = STRIP * q - HALO
        where = lane[: low_row.shape[0]]
        return jnp.where(
            where < 64, pltpu.roll(low_row, (-begin) % LANES, 1), pltpu.roll(high_row, (64 - begin) % LANES, 1)
        )

    has_low = (gy == 1).astype(F32)
    has_high = (gy == 0).astype(F32)

    def extended(own, edge, q):
        where = lane[: own.shape[0]]
        if q == 0:
            return jnp.where(where >= LANES - HALO, edge * has_low, own)
        if q == NX - 1:
            return jnp.where(where < HALO, edge * has_high, own)
        return own

    def row(ref, x):
        return ref[pl.ds(x, DOF, stride=8), :]

    def pack(own, edge, out, q):
        for i in range(4):
            parts = []
            for x in (i, i + 4):
                mine = row(own, x)
                parts.append(extended(mine, row(edge, x), q) if q in (0, NX - 1) else mine)
            out[q, 64 * i : 64 * i + 64, :] = window(parts[0], parts[1], q)

    def pack_mask(q):
        mine = fv[512:520, :]
        if q in (0, NX - 1):
            mine = extended(mine, f_edge[512:520, :], q)
        f_pack[q, 256:264, :] = window(mine, pltpu.roll(mine, 4, 0), q)

    g_swap = remote(gv, g_edge, edge_send.at[0], edge_recv.at[0], (tm, gx, 1 - gy))
    f_swap = remote(fv, f_edge, edge_send.at[1], edge_recv.at[1], (tm, gx, 1 - gy))

    def start_copy(q):
        return remote(g_pack.at[q], start.at[gx], start_send.at[q], start_recv.at[gx], (earlier, q, gy))

    def strip_copy(source, target, send, recv, q):
        return remote(source.at[q], target.at[gx], send.at[q], recv.at[gx], (tm, q, gy))

    def strip_send(source, target, send, recv, q):
        @pl.when(gx != q)
        def _():
            strip_copy(source, target, send, recv, q).start()

        @pl.when(gx == q)
        def _():
            pltpu.make_async_copy(source.at[q], target.at[gx], recv.at[gx]).start()

    def columns_copy(p):
        return remote(packed.at[p], gathered.at[tm], d_send, d_recv, (p, gx, gy))

    def e_copy(p):
        slot = (lax.rem(z, 2) * 4 + y) * NX + gx
        return remote(e_out.at[p], e_parts.at[slot], e_send, e_recv, (p, owner, gy))

    def finish():
        g_swap.wait_send()
        f_swap.wait_send()
        for q in range(NX):
            start_copy(q).wait_send()

            @pl.when(gx != q)
            def _():
                strip_copy(f_pack, strip_f, f_send, f_recv, q).wait_send()
                strip_copy(g_dense, strip_g, g_send, g_recv, q).wait_send()
        for q in range(NX):
            @pl.when(gx != q)
            def _():
                strip_copy(dense, res_parts, r_send, r_recv, q).wait_send()
        some = pl.ds(0, NT - 1)
        pltpu.make_async_copy(packed.at[some], gathered.at[some], d_send).wait()
        @pl.when(returns_here)
        def _():
            some = pl.ds(0, NT - 1)
            pltpu.make_async_copy(e_out.at[some], e_parts.at[some], e_send).wait()

        @pl.when(jnp.logical_not(returns_here))
        def _():
            pltpu.make_async_copy(e_out, e_parts, e_send).wait()

    for q in (1, 2):
        pack(gv, None, g_pack, q)
    pl.semaphore_wait(barrier, 18)
    for d in range(1, NY):
        pl.semaphore_signal(group_sem, inc=1, device_id=(lax.rem(y + d, NY) * NZ + z, gx, gy), device_id_type=MESH)
    g_swap.start()
    f_swap.start()
    for q in (1, 2):
        start_copy(q).start()
    for q in (1, 2):
        pack(fv, None, f_pack, q)
        pack_mask(q)
        strip_send(f_pack, strip_f, f_send, f_recv, q)
    g_swap.wait_recv()
    for q in (0, 3):
        pack(gv, g_edge, g_pack, q)
        start_copy(q).start()
    f_swap.wait_recv()
    for q in (0, 3):
        pack(fv, f_edge, f_pack, q)
        pack_mask(q)
        strip_send(f_pack, strip_f, f_send, f_recv, q)

    even_block = lax.rem(lane8 // STRIP, 2) == 0
    low_half = lane8 < 64

    def exchange(t):
        a = (
            jnp.where(low_half, t[0], pltpu.roll(t[2], 64, 1)),
            jnp.where(low_half, t[1], pltpu.roll(t[3], 64, 1)),
            jnp.where(low_half, pltpu.roll(t[0], 64, 1), t[2]),
            jnp.where(low_half, pltpu.roll(t[1], 64, 1), t[3]),
        )
        out = []
        for first, second in ((a[0], a[1]), (a[2], a[3])):
            out.append(jnp.where(even_block, first, pltpu.roll(second, STRIP, 1)))
            out.append(jnp.where(even_block, pltpu.roll(first, LANES - STRIP, 1), second))
        return out

    def place(h, b):
        return 2 * h + 4 * (b // 2) + b % 2

    for h in range(2):
        for v in range(8):
            rows = [
                gv[pl.ds(64 * v + place(h, b), 8, stride=8), :] * fv[512 + place(h, b) : 513 + place(h, b), :]
                for b in range(4)
            ]
            for q, tile in enumerate(exchange(rows)):
                g_dense[q, h, 8 * v : 8 * v + 8, :] = tile

    for load in matrix_loads:
        load.wait()
    left_operand(fine_op, pl.ds(0, 64), fine[...], temporary)
    left_operand(fine_op, pl.ds(64, 256), coupling[...], temporary)
    c1 = coarse[...]
    powers[0:64, :] = c1
    c2 = exact(c1, c1)
    powers[64:128, :] = c2
    powers[128:256, :] = exact(powers[0:128, :], c2)
    powers[256:512, :] = exact(powers[0:256, :], powers[192:256, :])
    c8 = powers[448:512, :]
    c16 = exact(c8, c8)
    left_operand(power_op, pl.ds(0, 512), powers[...], temporary)
    left_operand(power_op, pl.ds(512, 64), c16, temporary)

    is_last_interval = tm == NT - 1
    for q in range(NX):
        remote(g_pack.at[q], start.at[q], start_send.at[q], start_recv.at[q], (earlier, q, gy)).wait_recv()
        for i in range(4):
            begin = jnp.where(is_last_interval, 0.0, start[q, 64 * i : 64 * i + 64, :])
            high, low = split(begin)
            pair, half = 2 * q + i // 2, LANES * (i % 2)
            state[pair, 0:64, half : half + LANES] = high
            state[pair, 64:128, half : half + LANES] = low
    for q in range(NX):
        remote(f_pack.at[q], strip_f.at[q], f_send.at[q], f_recv.at[q], (tm, q, gy)).wait_recv()
        for i in range(4):
            mask_s[4 * q + i] = jnp.broadcast_to(strip_f[q, 256 + i : 257 + i, :], (8, LANES))

    def part(q, i, kind):
        half = LANES * (i % 2)
        return product[2 * q + i // 2, 64 * kind : 64 * kind + 64, half : half + LANES]

    for q in range(NX):
        strip_send(g_dense, strip_g, g_send, g_recv, q)

    def fine_step(k, final):
        for pair in range(8):
            rows = state[pair]
            product[pair] = mul(fine_op[...], jnp.concatenate([rows, rows], axis=0))
        scale = weight[k]
        low_lanes = lane < 64
        for q in range(NX):
            for i in range(4):
                if i > 0:
                    west = part(q, i - 1, 1)
                else:
                    before = part(q - 1, 3, 1) if q > 0 else jnp.zeros((64, LANES), F32)
                    west = pltpu.roll(jnp.where(low_lanes, part(q, 3, 1), before), 64, 1)
                if i < 3:
                    east = part(q, i + 1, 2)
                else:
                    after = part(q + 1, 0, 2) if q < NX - 1 else jnp.zeros((64, LANES), F32)
                    east = pltpu.roll(jnp.where(low_lanes, after, part(q, 0, 2)), 64, 1)
                south = pltpu.roll(part(q, i, 3), 1, 1)
                north = pltpu.roll(part(q, i, 4), LANES - 1, 1)
                value = (part(q, i, 0) + west) + (east + south) + (north + scale * strip_f[q, 64 * i : 64 * i + 64, :])
                mask = mask_s[4 * q + i]
                value = (value.reshape(8, 8, LANES) * mask[None]).reshape(64, LANES)
                if final:
                    last[4 * q + i] = value
                else:
                    high, low = split(value)
                    pair, half = 2 * q + i // 2, LANES * (i % 2)
                    state[pair, 0:64, half : half + LANES] = high
                    state[pair, 64:128, half : half + LANES] = low

    def body(step, carry):
        fine_step(STEPS - 1 - step, False)
        return carry

    lax.fori_loop(0, STEPS - 1, body, 0)
    fine_step(0, True)

    even_lanes = lax.rem(lane // STRIP, 2) == 0
    for q in range(NX):
        remote(g_dense.at[q], strip_g.at[q], g_send.at[q], g_recv.at[q], (tm, q, gy)).wait_recv()
        for h in range(2):
            tile = jnp.where(
                even_lanes, pltpu.roll(last[4 * q + 2 * h], LANES - HALO, 1), pltpu.roll(last[4 * q + 2 * h + 1], HALO, 1)
            ) - strip_g[q, h]
            dense[q, h] = tile
            for u in range(2):
                pieces = exchange([tile[8 * (2 * c + u) : 8 * (2 * c + u) + 8] for c in range(4)])
                for b in range(4):
                    packed[b * NZ + 2 * q + h, 8 * u : 8 * u + 8, :] = pieces[b]

    pl.semaphore_wait(group_sem, NY - 1)
    pltpu.make_async_copy(packed.at[tm], gathered.at[tm], d_recv).start()

    def send_columns(i, carry):
        columns_copy(lax.rem(tm + i, NT)).start()
        return carry

    lax.fori_loop(1, NT, send_columns, 0)
    for q in range(NX):
        strip_send(dense, res_parts, r_send, r_recv, q)

    pltpu.make_async_copy(packed, gathered, d_recv).wait()
    for k in range(NZ):
        for u in range(2):
            pieces = exchange([gathered[i * NZ + k, 8 * u : 8 * u + 8, :] for i in range(NY)])
            for c in range(4):
                scan[k, 8 * (2 * c + u) : 8 * (2 * c + u) + 8, :] = pieces[c]
    for k in range(1, NZ):
        terms = mul(power_op[0 : 64 * k, :], right_operand(scan[k]))
        for p in range(1, k + 1):
            scan_sum = terms[64 * (p - 1) : 64 * p, :]
            if p == k:
                sums[0] = (sums[0] if k > 1 else scan[0]) + scan_sum
            else:
                sums[k - p] = (sums[k - p] if p > 1 else scan[k - p]) + scan_sum
    total = sums[0]
    zero = jnp.zeros((64, LANES), F32)

    def from_later(d):
        return jnp.where(lane < LANES - STRIP * d, pltpu.roll(total, LANES - STRIP * d, 1), zero)

    entering = from_later(1) + mul(power_op[448:512, :], right_operand(from_later(2))) + mul(
        power_op[512:576, :], right_operand(from_later(3))
    )
    carried = mul(power_op[0:512, :], right_operand(entering))
    for k in range(NZ):
        local = sums[k] if k < NZ - 1 else scan[k]
        tile = local + carried[64 * (NZ - 1 - k) : 64 * (NZ - k), :]
        for u in range(2):
            pieces = exchange([tile[8 * (2 * c + u) : 8 * (2 * c + u) + 8] for c in range(4)])
            for i in range(NY):
                e_out[i * NZ + k, 8 * u : 8 * u + 8, :] = pieces[i]

    @pl.when(returns_here)
    def _():
        slot = (lax.rem(z, 2) * 4 + y) * NX + gx
        pltpu.make_async_copy(e_out.at[tm], e_parts.at[slot], e_recv).start()

    @pl.when(jnp.logical_not(returns_here))
    def _():
        e_copy(tm).start()

    def send_result(i, carry):
        e_copy(lax.rem(tm + i, NT)).start()
        return carry

    lax.fori_loop(1, NT, send_result, 0)

    for q in range(NX):
        remote(dense.at[q], res_parts.at[q], r_send.at[q], r_recv.at[q], (tm, q, gy)).wait_recv()
    for h in range(2):
        for v in range(8):
            tiles = exchange([res_parts[q, h, 8 * v : 8 * v + 8, :] for q in range(NX)])
            for b in range(4):
                res_v[pl.ds(64 * v + place(h, b), 8, stride=8), :] = tiles[b]

    pltpu.make_async_copy(e_out, e_parts, e_recv).wait()
    for h in range(2):
        for b in range(4):
            for u in range(2):
                tiles = exchange([e_parts[(4 * h + b) * NX + q, 8 * u : 8 * u + 8, :] for q in range(NX)])
                for c in range(4):
                    where = pl.ds(64 * (2 * c + u) + place(h, b), 8, stride=8)
                    upd_v[where, :] = gv[where, :] + tiles[c]

    finish()


def per_device(guesses, forcing, step_weight, land_mask, fine_matrix, coupling, coarse_matrix):
    vmem = pl.BlockSpec(memory_space=pltpu.VMEM)
    hbm = pl.BlockSpec(memory_space=pltpu.HBM)
    flat = jax.ShapeDtypeStruct((DOF * 8, LANES), F32)
    dma = pltpu.SemaphoreType.DMA
    updated, residual = pl.pallas_call(
        kernel,
        out_shape=(flat, flat),
        in_specs=[hbm, hbm, pl.BlockSpec(memory_space=pltpu.SMEM), hbm, hbm, hbm, hbm],
        out_specs=(vmem, vmem),
        scratch_shapes=[
            pltpu.VMEM((512, LANES), F32),
            pltpu.VMEM((520, LANES), F32),
            pltpu.VMEM((512, LANES), F32),
            pltpu.VMEM((520, LANES), F32),
            pltpu.VMEM((8, LANES), jnp.int32),
            pltpu.VMEM((NX, 256, LANES), F32),
            pltpu.VMEM((NX, 264, LANES), F32),
            pltpu.VMEM((NX, 256, LANES), F32),
            pltpu.VMEM((NX, 264, LANES), F32),
            pltpu.VMEM((NX, 2, 64, LANES), F32),
            pltpu.VMEM((16, 8, LANES), F32),
            pltpu.VMEM((NX, 2, 64, LANES), F32),
            pltpu.VMEM((320, 256), BF16),
            pltpu.VMEM((512, 256), F32),
            pltpu.VMEM((512, DOF), F32),
            pltpu.VMEM((576, 256), BF16),
            pltpu.VMEM((8, 128, 256), BF16),
            pltpu.VMEM((8, 320, 256), F32),
            pltpu.VMEM((16, 64, LANES), F32),
            pltpu.VMEM((NX, 2, 64, LANES), F32),
            pltpu.VMEM((NT, 16, LANES), F32),
            pltpu.VMEM((NT, 16, LANES), F32),
            pltpu.VMEM((NZ, 64, LANES), F32),
            pltpu.VMEM((NZ - 1, 64, LANES), F32),
            pltpu.VMEM((NT, 16, LANES), F32),
            pltpu.VMEM((NX, 2, 64, LANES), F32),
            pltpu.VMEM((NT, 16, LANES), F32),
            pltpu.VMEM((DOF, DOF), F32),
            pltpu.VMEM((4 * DOF, DOF), F32),
            pltpu.VMEM((DOF, DOF), F32),
            dma((6,)), dma((2,)), dma((2,)),
            dma((NX,)), dma((NX,)), dma((NX,)), dma((NX,)), dma((NX,)), dma((NX,)),
            dma, dma, dma((NX,)), dma((NX,)), dma, dma, pltpu.SemaphoreType.REGULAR,
        ],
        compiler_params=pltpu.CompilerParams(
            collective_id=0, has_side_effects=True, vmem_limit_bytes=60 * 1024 * 1024
        ),
    )(
        guesses.reshape(DOF * 8, LANES), forcing.reshape(DOF * 8, LANES), step_weight, land_mask,
        fine_matrix, coupling.reshape(4 * DOF, DOF), coarse_matrix,
    )
    return updated.reshape(guesses.shape), residual.reshape(guesses.shape)


def solution(mesh):
    tiles = P("tm", None, "gx", "gy")
    return jax.shard_map(
        per_device,
        mesh=mesh,
        in_specs=(tiles, tiles, P(), P("gx", "gy"), P(), P(), P()),
        out_specs=(tiles, tiles),
        check_vma=False,
    )
```

time: 66.8 us -> 64.1 us (0.960)
  local copies, waits for them, and re-layouts: 6.4 us -> 2.42 us
  Pallas kernels: 59 us -> 60.9 us
    unnamed x16 -> x4, local copies, waits for them, and re-layouts: 6.4 us -> 2.42 us
    pallas_call x1, Pallas kernels: 59 us -> 60.9 us  [per_device(): pl.pallas_call(kernel, out_shape=(flat, flat), in_specs=[hbm, hbm, pl.Blo...]
where the time goes in v2:
time: 64.1 us; the launch traced here: 64 us
  Pallas kernels  60.9 us (95%)
  local copies, waits for them, and re-layouts  2.42 us (4%)
  between operations  0.65 us (1%)
    pallas_call x1, Pallas kernels, per_device(): pl.pallas_call(kernel, out_shape=(flat, flat), in_specs=[hbm, hbm, pl.Blo...  60.9 us
    unnamed x4, local copies, waits for them, and re-layouts  2.42 us

profile of v2, /device:TPU:2, one launch (start us, length us, event | category | flops | bytes accessed | tf_op | source)
XLA Modules:
  0.0 64.0 jit_solution(3423456138582919260)
XLA Ops:
  0.6 60.9 %shard_map.86 = (f32[512,128]{1,0:T(8,128)}, f32[512,128]{1,0:T(8,128)}) custom-call(f32[512,128]{1,0:T(8,128)} %bitcast.5, f32[512,128]{1,0:T(8,128)} %bitcast.6, f32[16]{0:T(128)} %weight.1, s32[8,128]{1,0:T(8,128)} %mask_hbm.1, f32[64,64]{1,0:T(8,128)} %fine_hbm.1, f32[256,64]{1,0:T(8,128)} %bitcast.9, f32[64,64]{1,0:T(8,128)} %coarse_hbm.1), custom_call_target="tpu_custom_call" | custom-call | tf_op jit(solution)/shard_map/pallas_call | solution.py:407
  61.6 0.0 copy-start
  61.6 1.7 %copy.11 = f32[1,64,8,128]{3,2,1,0:T(8,128)} copy(f32[1,64,8,128]{3,2,1,0:T(8,128)} %bitcast.8) | data formatting | bytes 524288
  63.3 0.0 copy-done
  63.3 0.7 %copy.12 = f32[1,64,8,128]{3,2,1,0:T(8,128)} copy(f32[1,64,8,128]{3,2,1,0:T(8,128)S(1)} %bitcast.7) | data formatting | bytes 524288
Async XLA Ops:
  61.6 1.7 %copy-start = (f32[512,128]{1,0:T(8,128)S(1)}, f32[512,128]{1,0:T(8,128)}, u32[]{:S(2)}) copy-start(f32[512,128]{1,0:T(8,128)} %get-tuple-element.5) | copy-start | bytes 786436

commit v3 on v2

--- a/solution.py
+++ b/solution.py
@@ -53,7 +53,7 @@
 ):
     tm, gx, gy = lax.axis_index("tm"), lax.axis_index("gx"), lax.axis_index("gy")
     y, z = tm // NZ, lax.rem(tm, NZ)
-    owner = z // 2
+    owner = lax.rem(z // 2 + NX - gx, NX)
     returns_here = owner == gx
     lane = lax.broadcasted_iota(jnp.int32, (64, LANES), 1)
     lane8 = lax.broadcasted_iota(jnp.int32, (8, LANES), 1)
@@ -190,21 +190,25 @@
         pl.semaphore_signal(group_sem, inc=1, device_id=(lax.rem(y + d, NY) * NZ + z, gx, gy), device_id_type=MESH)
     g_swap.start()
     f_swap.start()
-    for q in (1, 2):
+    qa = 1 + lax.rem(gx, 2)
+    for q in (qa, 3 - qa):
+        start_copy(q).start()
+    g_swap.wait_recv()
+    for q in (0, 3):
+        pack(gv, g_edge, g_pack, q)
+    qc = 3 * lax.rem(gx, 2)
+    for q in (qc, 3 - qc):
         start_copy(q).start()
     for q in (1, 2):
         pack(fv, None, f_pack, q)
         pack_mask(q)
-        strip_send(f_pack, strip_f, f_send, f_recv, q)
-    g_swap.wait_recv()
-    for q in (0, 3):
-        pack(gv, g_edge, g_pack, q)
-        start_copy(q).start()
     f_swap.wait_recv()
     for q in (0, 3):
         pack(fv, f_edge, f_pack, q)
         pack_mask(q)
-        strip_send(f_pack, strip_f, f_send, f_recv, q)
+    for d in range(1, NX):
+        strip_copy(f_pack, strip_f, f_send, f_recv, lax.rem(gx + d, NX)).start()
+    pltpu.make_async_copy(f_pack.at[gx], strip_f.at[gx], f_recv.at[gx]).start()
 
     even_block = lax.rem(lane8 // STRIP, 2) == 0
     low_half = lane8 < 64
@@ -237,7 +241,8 @@
     for load in matrix_loads:
         load.wait()
     left_operand(fine_op, pl.ds(0, 64), fine[...], temporary)
-    left_operand(fine_op, pl.ds(64, 256), coupling[...], temporary)
+    left_operand(fine_op, pl.ds(64, 128), coupling[128:256, :], temporary)
+    left_operand(fine_op, pl.ds(192, 128), coupling[0:128, :], temporary)
     c1 = coarse[...]
     powers[0:64, :] = c1
     c2 = exact(c1, c1)
@@ -267,13 +272,19 @@
         half = LANES * (i % 2)
         return product[2 * q + i // 2, 64 * kind : 64 * kind + 64, half : half + LANES]
 
-    for q in range(NX):
-        strip_send(g_dense, strip_g, g_send, g_recv, q)
+    for d in range(1, NX):
+        strip_copy(g_dense, strip_g, g_send, g_recv, lax.rem(gx + d, NX)).start()
+    pltpu.make_async_copy(g_dense.at[gx], strip_g.at[gx], g_recv.at[gx]).start()
 
     def fine_step(k, final):
         for pair in range(8):
             rows = state[pair]
-            product[pair] = mul(fine_op[...], jnp.concatenate([rows, rows], axis=0))
+            terms = mul(fine_op[:, 0:192], jnp.concatenate([rows, rows[0:64]], axis=0))
+            for half in (slice(0, LANES), slice(LANES, 2 * LANES)):
+                south = pltpu.roll(terms[64:128, half], 1, 1)
+                north = pltpu.roll(terms[128:192, half], LANES - 1, 1)
+                product[pair, 0:64, half] = terms[0:64, half] + (south + north)
+            product[pair, 64:192] = terms[192:320]
         scale = weight[k]
         low_lanes = lane < 64
         for q in range(NX):
@@ -288,9 +299,7 @@
                 else:
                     after = part(q + 1, 0, 2) if q < NX - 1 else jnp.zeros((64, LANES), F32)
                     east = pltpu.roll(jnp.where(low_lanes, after, part(q, 0, 2)), 64, 1)
-                south = pltpu.roll(part(q, i, 3), 1, 1)
-                north = pltpu.roll(part(q, i, 4), LANES - 1, 1)
-                value = (part(q, i, 0) + west) + (east + south) + (north + scale * strip_f[q, 64 * i : 64 * i + 64, :])
+                value = (part(q, i, 0) + scale * strip_f[q, 64 * i : 64 * i + 64, :]) + (west + east)
                 mask = mask_s[4 * q + i]
                 value = (value.reshape(8, 8, LANES) * mask[None]).reshape(64, LANES)
                 if final:
@@ -319,7 +328,7 @@
             for u in range(2):
                 pieces = exchange([tile[8 * (2 * c + u) : 8 * (2 * c + u) + 8] for c in range(4)])
                 for b in range(4):
-                    packed[b * NZ + 2 * q + h, 8 * u : 8 * u + 8, :] = pieces[b]
+                    packed[b * NZ + 2 * lax.rem(q + gx, NX) + h, 8 * u : 8 * u + 8, :] = pieces[b]
 
     pl.semaphore_wait(group_sem, NY - 1)
     pltpu.make_async_copy(packed.at[tm], gathered.at[tm], d_recv).start()
@@ -329,8 +338,9 @@
         return carry
 
     lax.fori_loop(1, NT, send_columns, 0)
-    for q in range(NX):
-        strip_send(dense, res_parts, r_send, r_recv, q)
+    for d in range(1, NX):
+        strip_copy(dense, res_parts, r_send, r_recv, lax.rem(gx + d, NX)).start()
+    pltpu.make_async_copy(dense.at[gx], res_parts.at[gx], r_recv.at[gx]).start()
 
     pltpu.make_async_copy(packed, gathered, d_recv).wait()
     for k in range(NZ):
@@ -402,6 +412,10 @@
 def per_device(guesses, forcing, step_weight, land_mask, fine_matrix, coupling, coarse_matrix):
     vmem = pl.BlockSpec(memory_space=pltpu.VMEM)
     hbm = pl.BlockSpec(memory_space=pltpu.HBM)
+
+    def in_hbm(value):
+        return pltpu.with_memory_space_constraint(value, pltpu.HBM)
+
     flat = jax.ShapeDtypeStruct((DOF * 8, LANES), F32)
     dma = pltpu.SemaphoreType.DMA
     updated, residual = pl.pallas_call(
@@ -427,7 +441,7 @@
             pltpu.VMEM((512, DOF), F32),
             pltpu.VMEM((576, 256), BF16),
             pltpu.VMEM((8, 128, 256), BF16),
-            pltpu.VMEM((8, 320, 256), F32),
+            pltpu.VMEM((8, 192, 256), F32),
             pltpu.VMEM((16, 64, LANES), F32),
             pltpu.VMEM((NX, 2, 64, LANES), F32),
             pltpu.VMEM((NT, 16, LANES), F32),
@@ -445,11 +459,11 @@
             dma, dma, dma((NX,)), dma((NX,)), dma, dma, pltpu.SemaphoreType.REGULAR,
         ],
         compiler_params=pltpu.CompilerParams(
-            collective_id=0, has_side_effects=True, vmem_limit_bytes=60 * 1024 * 1024
+            collective_id=0, has_side_effects=True, vmem_limit_bytes=24 * 1024 * 1024
         ),
     )(
-        guesses.reshape(DOF * 8, LANES), forcing.reshape(DOF * 8, LANES), step_weight, land_mask,
-        fine_matrix, coupling.reshape(4 * DOF, DOF), coarse_matrix,
+        in_hbm(guesses.reshape(DOF * 8, LANES)), in_hbm(forcing.reshape(DOF * 8, LANES)), step_weight, in_hbm(land_mask),
+        in_hbm(fine_matrix), in_hbm(coupling.reshape(4 * DOF, DOF)), in_hbm(coarse_matrix),
     )
     return updated.reshape(guesses.shape), residual.reshape(guesses.shape)
 

time: 64.1 us -> 59.4 us (0.927)
  Pallas kernels: 60.9 us -> 56.3 us
    pallas_call x1, Pallas kernels: 60.9 us -> 56.3 us  [per_device(): pl.pallas_call(kernel, out_shape=(flat, flat), in_specs=[hbm, hbm, pl.Blo...]
where the time goes in v3:
time: 59.4 us; the launch traced here: 59 us
  Pallas kernels  56.3 us (95%)
  local copies, waits for them, and re-layouts  2.06 us (3%)
  between operations  0.65 us (1%)
    pallas_call x1, Pallas kernels, per_device(): pl.pallas_call(kernel, out_shape=(flat, flat), in_specs=[hbm, hbm, pl.Blo...  56.3 us
    unnamed x4, local copies, waits for them, and re-layouts  2.06 us

profile of v3, /device:TPU:2, one launch (start us, length us, event | category | flops | bytes accessed | tf_op | source)
XLA Modules:
  0.0 59.0 jit_solution(7443402467695676588)
XLA Ops:
  0.6 0.0 copy-start
  0.6 0.6 %copy-done = f32[16]{0:T(128)S(1)} copy-done((f32[16]{0:T(128)S(1)}, f32[16]{0:T(128)}, u32[]{:S(2)}) %copy-start) | copy-done | bytes 88
  1.3 56.3 %shard_map.86 = (f32[512,128]{1,0:T(8,128)S(1)}, f32[512,128]{1,0:T(8,128)S(1)}) custom-call(f32[512,128]{1,0:T(8,128)} %bitcast.7, f32[512,128]{1,0:T(8,128)} %bitcast.8, f32[16]{0:T(128)S(1)} %copy-done, s32[8,128]{1,0:T(8,128)} %mask_hbm.1, f32[64,64]{1,0:T(8,128)} %fine_hbm.1, f32[256,64]{1,0:T(8,128)} %bitcast.9, f32[64,64]{1,0:T(8,128)} %coarse_hbm.1), custom_call_target="tpu_custom_call" | custom-call | tf_op jit(solution)/shard_map/pallas_call | solution.py:421
  57.6 0.7 %copy.11 = f32[1,64,8,128]{3,2,1,0:T(8,128)} copy(f32[1,64,8,128]{3,2,1,0:T(8,128)S(1)} %bitcast.6) | data formatting | bytes 524288
  58.3 0.7 %copy.12 = f32[1,64,8,128]{3,2,1,0:T(8,128)} copy(f32[1,64,8,128]{3,2,1,0:T(8,128)S(1)} %bitcast.5) | data formatting | bytes 524288
Async XLA Ops:
  0.6 0.7 %copy-start = (f32[16]{0:T(128)S(1)}, f32[16]{0:T(128)}, u32[]{:S(2)}) copy-start(f32[16]{0:T(128)} %weight.1) | copy-start | bytes 196

commit v4 on v3

--- a/solution.py
+++ b/solution.py
@@ -277,7 +277,10 @@
     pltpu.make_async_copy(g_dense.at[gx], strip_g.at[gx], g_recv.at[gx]).start()
 
     def fine_step(k, final):
-        for pair in range(8):
+        scale = weight[k]
+        low_lanes = lane < 64
+
+        def multiply(pair):
             rows = state[pair]
             terms = mul(fine_op[:, 0:192], jnp.concatenate([rows, rows[0:64]], axis=0))
             for half in (slice(0, LANES), slice(LANES, 2 * LANES)):
@@ -285,9 +288,8 @@
                 north = pltpu.roll(terms[128:192, half], LANES - 1, 1)
                 product[pair, 0:64, half] = terms[0:64, half] + (south + north)
             product[pair, 64:192] = terms[192:320]
-        scale = weight[k]
-        low_lanes = lane < 64
-        for q in range(NX):
+
+        def combine(q):
             for i in range(4):
                 if i > 0:
                     west = part(q, i - 1, 1)
@@ -310,11 +312,17 @@
                     state[pair, 0:64, half : half + LANES] = high
                     state[pair, 64:128, half : half + LANES] = low
 
+        for pair in range(8):
+            multiply(pair)
+            if pair % 2 == 0 and pair > 0:
+                combine(pair // 2 - 1)
+        combine(NX - 1)
+
     def body(step, carry):
         fine_step(STEPS - 1 - step, False)
         return carry
 
-    lax.fori_loop(0, STEPS - 1, body, 0)
+    lax.fori_loop(0, STEPS - 1, body, 0, unroll=5)
     fine_step(0, True)
 
     even_lanes = lax.rem(lane // STRIP, 2) == 0

time: 59.4 us -> 57.6 us (0.970)
  Pallas kernels: 56.3 us -> 54.5 us
    pallas_call x1, Pallas kernels: 56.3 us -> 54.5 us  [per_device(): pl.pallas_call(kernel, out_shape=(flat, flat), in_specs=[hbm, hbm, pl.Blo...]
where the time goes in v4:
time: 57.6 us; the launch traced here: 57.2 us
  Pallas kernels  54.5 us (95%)
  local copies, waits for them, and re-layouts  2.06 us (4%)
  between operations  0.65 us (1%)
    pallas_call x1, Pallas kernels, per_device(): pl.pallas_call(kernel, out_shape=(flat, flat), in_specs=[hbm, hbm, pl.Blo...  54.5 us
    unnamed x4, local copies, waits for them, and re-layouts  2.06 us

profile of v4, /device:TPU:2, one launch (start us, length us, event | category | flops | bytes accessed | tf_op | source)
XLA Modules:
  0.0 57.2 jit_solution(11765750054102053849)
XLA Ops:
  0.6 0.0 copy-start
  0.6 0.6 %copy-done = f32[16]{0:T(128)S(1)} copy-done((f32[16]{0:T(128)S(1)}, f32[16]{0:T(128)}, u32[]{:S(2)}) %copy-start) | copy-done | bytes 88
  1.3 54.5 %shard_map.86 = (f32[512,128]{1,0:T(8,128)S(1)}, f32[512,128]{1,0:T(8,128)S(1)}) custom-call(f32[512,128]{1,0:T(8,128)} %bitcast.7, f32[512,128]{1,0:T(8,128)} %bitcast.8, f32[16]{0:T(128)S(1)} %copy-done, s32[8,128]{1,0:T(8,128)} %mask_hbm.1, f32[64,64]{1,0:T(8,128)} %fine_hbm.1, f32[256,64]{1,0:T(8,128)} %bitcast.9, f32[64,64]{1,0:T(8,128)} %coarse_hbm.1), custom_call_target="tpu_custom_call" | custom-call | tf_op jit(solution)/shard_map/pallas_call | solution.py:429
  55.7 0.7 %copy.11 = f32[1,64,8,128]{3,2,1,0:T(8,128)} copy(f32[1,64,8,128]{3,2,1,0:T(8,128)S(1)} %bitcast.6) | data formatting | bytes 524288
  56.5 0.7 %copy.12 = f32[1,64,8,128]{3,2,1,0:T(8,128)} copy(f32[1,64,8,128]{3,2,1,0:T(8,128)S(1)} %bitcast.5) | data formatting | bytes 524288
Async XLA Ops:
  0.6 0.7 %copy-start = (f32[16]{0:T(128)S(1)}, f32[16]{0:T(128)}, u32[]{:S(2)}) copy-start(f32[16]{0:T(128)} %weight.1) | copy-start | bytes 196

commit v5 on v4

--- a/solution.py
+++ b/solution.py
@@ -322,7 +322,7 @@
         fine_step(STEPS - 1 - step, False)
         return carry
 
-    lax.fori_loop(0, STEPS - 1, body, 0, unroll=5)
+    lax.fori_loop(0, STEPS - 1, body, 0, unroll=15)
     fine_step(0, True)
 
     even_lanes = lax.rem(lane // STRIP, 2) == 0

time: 57.6 us -> 56.8 us (0.986)
  Pallas kernels: 54.5 us -> 53.7 us
    pallas_call x1, Pallas kernels: 54.5 us -> 53.7 us  [per_device(): pl.pallas_call(kernel, out_shape=(flat, flat), in_specs=[hbm, hbm, pl.Blo...]
where the time goes in v5:
time: 56.8 us; the launch traced here: 56.4 us
  Pallas kernels  53.7 us (95%)
  local copies, waits for them, and re-layouts  2.06 us (4%)
  between operations  0.65 us (1%)
    pallas_call x1, Pallas kernels, per_device(): pl.pallas_call(kernel, out_shape=(flat, flat), in_specs=[hbm, hbm, pl.Blo...  53.7 us
    unnamed x4, local copies, waits for them, and re-layouts  2.06 us

profile of v5, /device:TPU:2, one launch (start us, length us, event | category | flops | bytes accessed | tf_op | source)
XLA Modules:
  0.0 56.4 jit_solution(9168080723639464103)
XLA Ops:
  0.6 0.0 copy-start
  0.6 0.6 %copy-done = f32[16]{0:T(128)S(1)} copy-done((f32[16]{0:T(128)S(1)}, f32[16]{0:T(128)}, u32[]{:S(2)}) %copy-start) | copy-done | bytes 88
  1.3 53.7 %shard_map.86 = (f32[512,128]{1,0:T(8,128)S(1)}, f32[512,128]{1,0:T(8,128)S(1)}) custom-call(f32[512,128]{1,0:T(8,128)} %bitcast.7, f32[512,128]{1,0:T(8,128)} %bitcast.8, f32[16]{0:T(128)S(1)} %copy-done, s32[8,128]{1,0:T(8,128)} %mask_hbm.1, f32[64,64]{1,0:T(8,128)} %fine_hbm.1, f32[256,64]{1,0:T(8,128)} %bitcast.9, f32[64,64]{1,0:T(8,128)} %coarse_hbm.1), custom_call_target="tpu_custom_call" | custom-call | tf_op jit(solution)/shard_map/pallas_call | solution.py:429
  55.0 0.7 %copy.11 = f32[1,64,8,128]{3,2,1,0:T(8,128)} copy(f32[1,64,8,128]{3,2,1,0:T(8,128)S(1)} %bitcast.6) | data formatting | bytes 524288
  55.7 0.7 %copy.12 = f32[1,64,8,128]{3,2,1,0:T(8,128)} copy(f32[1,64,8,128]{3,2,1,0:T(8,128)S(1)} %bitcast.5) | data formatting | bytes 524288
Async XLA Ops:
  0.6 0.7 %copy-start = (f32[16]{0:T(128)S(1)}, f32[16]{0:T(128)}, u32[]{:S(2)}) copy-start(f32[16]{0:T(128)} %weight.1) | copy-start | bytes 196

commit v6 on v5

--- a/solution.py
+++ b/solution.py
@@ -326,26 +326,27 @@
     fine_step(0, True)
 
     even_lanes = lax.rem(lane // STRIP, 2) == 0
+    pl.semaphore_wait(group_sem, NY - 1)
     for q in range(NX):
         remote(g_dense.at[q], strip_g.at[q], g_send.at[q], g_recv.at[q], (tm, q, gy)).wait_recv()
-        for h in range(2):
-            tile = jnp.where(
-                even_lanes, pltpu.roll(last[4 * q + 2 * h], LANES - HALO, 1), pltpu.roll(last[4 * q + 2 * h + 1], HALO, 1)
-            ) - strip_g[q, h]
-            dense[q, h] = tile
-            for u in range(2):
-                pieces = exchange([tile[8 * (2 * c + u) : 8 * (2 * c + u) + 8] for c in range(4)])
-                for b in range(4):
-                    packed[b * NZ + 2 * lax.rem(q + gx, NX) + h, 8 * u : 8 * u + 8, :] = pieces[b]
-
-    pl.semaphore_wait(group_sem, NY - 1)
-    pltpu.make_async_copy(packed.at[tm], gathered.at[tm], d_recv).start()
-
-    def send_columns(i, carry):
-        columns_copy(lax.rem(tm + i, NT)).start()
-        return carry
-
-    lax.fori_loop(1, NT, send_columns, 0)
+    for n in (4, 3, 5, 2, 6, 1, 7, 0):
+        k = lax.rem(z + n, NZ)
+        q, h = lax.rem(k // 2 + NX - gx, NX), lax.rem(k, 2)
+        tile = jnp.where(
+            even_lanes, pltpu.roll(last[4 * q + 2 * h], LANES - HALO, 1), pltpu.roll(last[4 * q + 2 * h + 1], HALO, 1)
+        ) - strip_g[q, h]
+        dense[q, h] = tile
+        for u in range(2):
+            pieces = exchange([tile[8 * (2 * c + u) : 8 * (2 * c + u) + 8] for c in range(4)])
+            for b in range(4):
+                packed[b * NZ + k, 8 * u : 8 * u + 8, :] = pieces[b]
+        for b in range(4):
+            p = lax.rem(y + b, NY) * NZ + k
+            if b == 0 and n == 0:
+                pltpu.make_async_copy(packed.at[tm], gathered.at[tm], d_recv).start()
+            else:
+                columns_copy(p).start()
+
     for d in range(1, NX):
         strip_copy(dense, res_parts, r_send, r_recv, lax.rem(gx + d, NX)).start()
     pltpu.make_async_copy(dense.at[gx], res_parts.at[gx], r_recv.at[gx]).start()

time: 56.8 us -> 56.5 us (level); the launches traced: 56.4 us -> 55.4 us
  Pallas kernels: 53.7 us -> 52.7 us
    pallas_call x1, Pallas kernels: 53.7 us -> 52.7 us  [per_device(): pl.pallas_call(kernel, out_shape=(flat, flat), in_specs=[hbm, hbm, pl.Blo...]
where the time goes in v6:
time: 56.5 us; the launch traced here: 55.4 us
  Pallas kernels  52.7 us (93%)
  local copies, waits for them, and re-layouts  2.06 us (4%)
  between operations  0.65 us (1%)
    pallas_call x1, Pallas kernels, per_device(): pl.pallas_call(kernel, out_shape=(flat, flat), in_specs=[hbm, hbm, pl.Blo...  52.7 us
    unnamed x4, local copies, waits for them, and re-layouts  2.06 us

profile of v6, /device:TPU:2, one launch (start us, length us, event | category | flops | bytes accessed | tf_op | source)
XLA Modules:
  0.0 55.4 jit_solution(1392211967326105291)
XLA Ops:
  0.6 0.0 copy-start
  0.6 0.6 %copy-done = f32[16]{0:T(128)S(1)} copy-done((f32[16]{0:T(128)S(1)}, f32[16]{0:T(128)}, u32[]{:S(2)}) %copy-start) | copy-done | bytes 88
  1.3 52.7 %shard_map.86 = (f32[512,128]{1,0:T(8,128)S(1)}, f32[512,128]{1,0:T(8,128)S(1)}) custom-call(f32[512,128]{1,0:T(8,128)} %bitcast.7, f32[512,128]{1,0:T(8,128)} %bitcast.8, f32[16]{0:T(128)S(1)} %copy-done, s32[8,128]{1,0:T(8,128)} %mask_hbm.1, f32[64,64]{1,0:T(8,128)} %fine_hbm.1, f32[256,64]{1,0:T(8,128)} %bitcast.9, f32[64,64]{1,0:T(8,128)} %coarse_hbm.1), custom_call_target="tpu_custom_call" | custom-call | tf_op jit(solution)/shard_map/pallas_call | solution.py:430
  54.0 0.7 %copy.11 = f32[1,64,8,128]{3,2,1,0:T(8,128)} copy(f32[1,64,8,128]{3,2,1,0:T(8,128)S(1)} %bitcast.6) | data formatting | bytes 524288
  54.7 0.7 %copy.12 = f32[1,64,8,128]{3,2,1,0:T(8,128)} copy(f32[1,64,8,128]{3,2,1,0:T(8,128)S(1)} %bitcast.5) | data formatting | bytes 524288
Async XLA Ops:
  0.6 0.7 %copy-start = (f32[16]{0:T(128)S(1)}, f32[16]{0:T(128)}, u32[]{:S(2)}) copy-start(f32[16]{0:T(128)} %weight.1) | copy-start | bytes 196
